TPU v7x, 32 devices: a whole 2x2x4 slice. The times are simulated.
32 devices in a mesh: fsdp: 8 (over z, x), seq: 4 (over y, core).
Axes of the slice: x: 2, y: 2, z: 4, core: 2. Of those that a mesh axis runs over, the one named last changes fastest.
Arguments:
- layer_input: bfloat16 [8192, 768], P(('fsdp', 'seq')), may hold values from -6 to 6
- out_grad: bfloat16 [8192, 768], P(('fsdp', 'seq')), may hold values from -6 to 6
- doc_ids: int32 [8192], replicated, may hold values from 0 to 2, as said below
- w_qkv: float32 [768, 2304], P('fsdp'), may hold values from -0.21875 to 0.21875
- w_out: float32 [768, 768], P('fsdp'), may hold values from -12 to 12
- norm1_gain: float32 [768], P('fsdp'), may hold values from 0.25 to 1.75
- norm1_bias: float32 [768], P('fsdp'), may hold values from -1.75 to 1.75
- w_up: float32 [768, 3072], P('fsdp'), may hold values from -0.21875 to 0.21875
- w_gate: float32 [768, 3072], P('fsdp'), may hold values from -0.21875 to 0.21875
- w_down: float32 [3072, 768], P('fsdp'), may hold values from -0.109375 to 0.109375
- norm2_gain: float32 [768], P('fsdp'), may hold values from 0.25 to 1.75
- norm2_bias: float32 [768], P('fsdp'), may hold values from -1.75 to 1.75
Outputs:
- output: bfloat16 [8192, 768], P(('fsdp', 'seq'))
- input_grad: bfloat16 [8192, 768], P(('fsdp', 'seq'))
- grad_w_qkv: float32 [768, 2304], P('fsdp')
- grad_w_out: float32 [768, 768], P('fsdp')
- grad_norm1_gain: float32 [768], P('fsdp')
- grad_norm1_bias: float32 [768], P('fsdp')
- grad_w_up: float32 [768, 3072], P('fsdp')
- grad_w_gate: float32 [768, 3072], P('fsdp')
- grad_w_down: float32 [3072, 768], P('fsdp')
- grad_norm2_gain: float32 [768], P('fsdp')
- grad_norm2_bias: float32 [768], P('fsdp')
Inputs may be any that keep to these rules, and one draw needn't show every extreme that they name: `doc_ids`: ids never fall along the tokens. Sequence s (tokens s * 8192 to (s + 1) * 8192 - 1) holds exactly three documents, numbered 3 s, 3 s + 1 and 3 s + 2; its first document ends within its first 1024 tokens and its last one begins within its last 1024 tokens.
All inputs are finite; a program needn't handle non-finite values.
Results may differ from a plain program's by a relative error of at most 0.025.
Values may be sent and summed in bfloat16 or wider, within the bound.
No kernel may reach another device: no remote copies, remote signals or barrier semaphores. Data moves between devices by JAX's collectives and lax.ppermute only.
A program may use at most 128 MiB of HBM per device.

v0:
```python
import math

import jax
import jax.numpy as jnp
from jax import lax
from jax.sharding import PartitionSpec as P

HEADS = 12
HEAD_DIM = 64
SPAN = 8


norm_eps = 1e-12
base_log = math.log(1000.0)
masked = -1e30


def swapped(value, axis, stride):
    mask = 2**stride
    pairs = [(source, source ^ mask) for source in range(lax.axis_size(axis))]
    return lax.ppermute(value, axis, pairs)


def rotate(field, cosine_table, sine_table):
    half_dim = field.shape[-1] // 2
    lead_half = field[..., :half_dim]
    tail_half = field[..., half_dim:]
    return jnp.concatenate(
        [
            lead_half * cosine_table - tail_half * sine_table,
            tail_half * cosine_table + lead_half * sine_table,
        ],
        axis=-1,
    )


def tables(positions, head_size):
    steps = jnp.arange(head_size // 2, dtype=jnp.float32)
    freqs = jnp.exp(steps * (-2.0 * base_log / head_size))
    angles = positions.astype(jnp.float32)[:, None] * freqs[None, :]
    return (jnp.cos(angles)[:, None, :], jnp.sin(angles)[:, None, :])


def normalize(rows_in, gain, bias):
    centre = rows_in - jnp.mean(rows_in, axis=-1, keepdims=True)
    spread = jnp.mean(centre * centre, axis=-1, keepdims=True)
    return centre * lax.rsqrt(spread + norm_eps) * gain + bias


def swiglu(gate_act, up_act):
    return gate_act * lax.logistic(gate_act) * up_act


def product(left_op, right_op):
    return jnp.dot(left_op, right_op, preferred_element_type=jnp.float32)


def left_product(left_op, right_op):
    return lax.dot_general(
        left_op, right_op, (((0,), (0,)), ((), ())), preferred_element_type=jnp.float32
    )


def right_product(left_op, right_op):
    return lax.dot_general(
        left_op, right_op, (((1,), (1,)), ((), ())), preferred_element_type=jnp.float32
    )


def over_blocks(carry_in, portion, offset, seq_lower, seq_upper, step_fn):
    row_count = portion.shape[1]
    blk_rows = 512

    def one_turn(turn_index, carry_now):
        key_first = offset + turn_index * blk_rows
        sub_block = lax.dynamic_slice_in_dim(portion, turn_index * blk_rows, blk_rows, 1)
        inside = jnp.logical_and(key_first < seq_upper, key_first + blk_rows > seq_lower)
        return lax.cond(
            inside,
            lambda carry_arg: step_fn(carry_arg, sub_block, key_first),
            lambda carry_arg: carry_arg,
            carry_now,
        )

    return lax.fori_loop(0, row_count // blk_rows, one_turn, carry_in)


def fold_peers(stacked, fold_fn, initial):
    shard_rows = stacked.shape[1]
    fsdp_here = lax.axis_index("fsdp")
    result = fold_fn(initial, stacked, fsdp_here * shard_rows)
    collected = stacked
    level_count = SPAN.bit_length() - 1
    for level in range(level_count):
        partner = swapped(collected, "fsdp", level)
        partner_first = (fsdp_here >> level ^ 1) << level
        result = fold_fn(result, partner, partner_first * shard_rows)
        if level + 1 < level_count:
            lower_half = fsdp_here >> level & 1 == 0
            collected = jnp.where(
                lower_half,
                jnp.concatenate([collected, partner], axis=1),
                jnp.concatenate([partner, collected], axis=1),
            )
    return result


def local(
    layer_input,
    out_grad,
    doc_ids,
    w_qkv,
    w_out,
    norm1_gain,
    norm1_bias,
    w_up,
    w_gate,
    w_down,
    norm2_gain,
    norm2_bias,
):
    gathered = (
        lax.all_gather(w_qkv.astype(jnp.bfloat16), "fsdp", axis=0, tiled=True),
        lax.all_gather(w_out.astype(jnp.bfloat16), "fsdp", axis=0, tiled=True),
        lax.all_gather(norm1_gain.astype(jnp.bfloat16), "fsdp", axis=0, tiled=True),
        lax.all_gather(norm1_bias.astype(jnp.bfloat16), "fsdp", axis=0, tiled=True),
        lax.all_gather(w_up.astype(jnp.bfloat16), "fsdp", axis=0, tiled=True),
        lax.all_gather(w_gate.astype(jnp.bfloat16), "fsdp", axis=0, tiled=True),
        lax.all_gather(w_down.astype(jnp.bfloat16), "fsdp", axis=0, tiled=True),
        lax.all_gather(norm2_gain.astype(jnp.bfloat16), "fsdp", axis=0, tiled=True),
        lax.all_gather(norm2_bias.astype(jnp.bfloat16), "fsdp", axis=0, tiled=True),
    )
    (
        qkv_full,
        out_full,
        gain1_low,
        bias1_low,
        up_full,
        gate_full,
        down_full,
        gain2_low,
        bias2_low,
    ) = gathered
    gain_one = gain1_low.astype(jnp.float32)
    bias_one = bias1_low.astype(jnp.float32)
    gain_two = gain2_low.astype(jnp.float32)
    bias_two = bias2_low.astype(jnp.float32)
    tok_rows, model_width = layer_input.shape
    groups = lax.axis_size("seq")
    heads_dev = HEADS // groups
    inner_width = heads_dev * HEAD_DIM
    group_rows = tok_rows * groups
    length = SPAN * group_rows
    fsdp_here = lax.axis_index("fsdp")
    row_first = (fsdp_here * groups + lax.axis_index("seq")) * tok_rows
    positions = (row_first + jnp.arange(tok_rows, dtype=jnp.int32)) % length
    cosine_table, sine_table = tables(positions, HEAD_DIM)
    score_scale = HEAD_DIM ** (-0.5)
    projected = product(layer_input, qkv_full)
    raw_queries = projected[:, :model_width].reshape(tok_rows, HEADS, HEAD_DIM)
    raw_keys = projected[:, model_width : 2 * model_width].reshape(tok_rows, HEADS, HEAD_DIM)

    def turn_both(query_part, key_part):
        return (
            rotate(query_part, cosine_table, sine_table),
            rotate(key_part, cosine_table, sine_table),
        )

    turned, unturn = jax.vjp(turn_both, raw_queries, raw_keys)
    stacked = jnp.stack(
        [
            turned[0].reshape(tok_rows, model_width).astype(jnp.bfloat16),
            turned[1].reshape(tok_rows, model_width).astype(jnp.bfloat16),
            projected[:, 2 * model_width :].astype(jnp.bfloat16),
        ]
    )
    stacked = stacked.reshape(3, tok_rows, groups, inner_width)
    regrouped = lax.all_to_all(stacked, "seq", split_axis=2, concat_axis=1, tiled=True).reshape(
        3, group_rows, inner_width
    )
    queries = regrouped[0].reshape(group_rows, heads_dev, HEAD_DIM)
    own_keys = regrouped[1].reshape(group_rows, heads_dev, HEAD_DIM)
    own_values = regrouped[2].reshape(group_rows, heads_dev, HEAD_DIM)
    keys_values = regrouped[1:]
    seq_lower = fsdp_here // SPAN * length
    seq_upper = seq_lower + length
    own_docs = lax.dynamic_slice_in_dim(doc_ids, fsdp_here * group_rows, group_rows)

    def score_pair(query_block, key_block, query_docs, key_docs):
        scores = (
            jnp.einsum("qhd,khd->qhk", query_block, key_block, preferred_element_type=jnp.float32)
            * score_scale
        )
        allowed = (query_docs[:, None] == key_docs[None, :])[:, None, :]
        return (scores, allowed)

    def forward_step(carry_now, sub_block, key_first):
        row_top, row_sum, weighted = carry_now
        key_block = sub_block[0].reshape(-1, heads_dev, HEAD_DIM)
        value_block = sub_block[1].reshape(-1, heads_dev, HEAD_DIM)
        key_docs = lax.dynamic_slice_in_dim(doc_ids, key_first, sub_block.shape[1])
        scores, allowed = score_pair(queries, key_block, own_docs, key_docs)
        scores = jnp.where(allowed, scores, masked)
        new_top = jnp.maximum(row_top, jnp.max(scores, axis=-1))
        weights = jnp.where(allowed, jnp.exp(scores - new_top[..., None]), 0.0)
        factor = jnp.exp(row_top - new_top)
        row_sum = row_sum * factor + jnp.sum(weights, axis=-1)
        weighted = weighted * factor[..., None] + jnp.einsum(
            "qhk,khd->qhd",
            weights.astype(jnp.bfloat16),
            value_block,
            preferred_element_type=jnp.float32,
        )
        return (new_top, row_sum, weighted)

    def forward_fold(carry_now, portion, offset):
        return over_blocks(carry_now, portion, offset, seq_lower, seq_upper, forward_step)

    start_state = (
        jnp.full((group_rows, heads_dev), masked, jnp.float32),
        jnp.zeros((group_rows, heads_dev), jnp.float32),
        jnp.zeros((group_rows, heads_dev, HEAD_DIM), jnp.float32),
    )
    row_top, row_sum, weighted = fold_peers(keys_values, forward_fold, start_state)
    attn_out = weighted / row_sum[..., None]
    log_total = row_top + jnp.log(row_sum)
    attn_low = attn_out.astype(jnp.bfloat16).reshape(group_rows, 1, inner_width)
    head_tokens = lax.all_to_all(attn_low, "seq", split_axis=0, concat_axis=1, tiled=True).reshape(
        tok_rows, model_width
    )
    first_sum = layer_input.astype(jnp.float32) + product(head_tokens, out_full)
    hidden, norm1_back = jax.vjp(normalize, first_sum, gain_one, bias_one)
    hidden_low = hidden.astype(jnp.bfloat16)
    up_act = product(hidden_low, up_full)
    gate_act = product(hidden_low, gate_full)
    inner_act, swiglu_back = jax.vjp(swiglu, gate_act, up_act)
    inner_low = inner_act.astype(jnp.bfloat16)
    second_sum = hidden + product(inner_low, down_full)
    result, norm2_back = jax.vjp(normalize, second_sum, gain_two, bias_two)
    d_second, grad_gain_two, grad_bias_two = norm2_back(out_grad.astype(jnp.float32))
    d_branch_two = d_second.astype(jnp.bfloat16)
    grad_down = left_product(inner_low, d_branch_two)
    d_inner = right_product(d_branch_two, down_full)
    d_gate, d_up = swiglu_back(d_inner)
    d_gate_low = d_gate.astype(jnp.bfloat16)
    d_up_low = d_up.astype(jnp.bfloat16)
    grad_up = left_product(hidden_low, d_up_low)
    grad_gate = left_product(hidden_low, d_gate_low)
    d_hidden = d_second + right_product(d_up_low, up_full) + right_product(d_gate_low, gate_full)
    d_first, grad_gain_one, grad_bias_one = norm1_back(d_hidden)
    d_branch_one = d_first.astype(jnp.bfloat16)
    grad_out = left_product(head_tokens, d_branch_one)
    d_tokens = right_product(d_branch_one, out_full).astype(jnp.bfloat16)
    d_heads = lax.all_to_all(
        d_tokens.reshape(tok_rows, groups, inner_width),
        "seq",
        split_axis=1,
        concat_axis=0,
        tiled=True,
    )
    d_heads = d_heads.reshape(group_rows, heads_dev, HEAD_DIM)
    row_delta = jnp.sum(d_heads.astype(jnp.float32) * attn_out, axis=-1)
    all_lse, all_delta = (
        lax.all_gather(log_total, "fsdp", axis=0, tiled=True),
        lax.all_gather(row_delta, "fsdp", axis=0, tiled=True),
    )

    def query_grad_step(d_query_sum, sub_block, key_first):
        key_block = sub_block[0].reshape(-1, heads_dev, HEAD_DIM)
        value_block = sub_block[1].reshape(-1, heads_dev, HEAD_DIM)
        key_docs = lax.dynamic_slice_in_dim(doc_ids, key_first, sub_block.shape[1])
        scores, allowed = score_pair(queries, key_block, own_docs, key_docs)
        weights = jnp.where(allowed, jnp.exp(scores - log_total[..., None]), 0.0)
        d_weights = jnp.einsum(
            "qhd,khd->qhk", d_heads, value_block, preferred_element_type=jnp.float32
        )
        d_scores = (weights * (d_weights - row_delta[..., None])).astype(jnp.bfloat16)
        return d_query_sum + jnp.einsum(
            "qhk,khd->qhd", d_scores, key_block, preferred_element_type=jnp.float32
        )

    def query_grad_fold(carry_now, portion, offset):
        return over_blocks(carry_now, portion, offset, seq_lower, seq_upper, query_grad_step)

    d_queries = (
        fold_peers(
            keys_values, query_grad_fold, jnp.zeros((group_rows, heads_dev, HEAD_DIM), jnp.float32)
        )
        * score_scale
    )

    def key_grad_step(carry_now, sub_block, query_first):
        d_key_sum, d_value_sum = carry_now
        query_block = sub_block[0].reshape(-1, heads_dev, HEAD_DIM)
        grad_block = sub_block[1].reshape(-1, heads_dev, HEAD_DIM)
        row_count = sub_block.shape[1]
        lse_rows = lax.dynamic_slice_in_dim(all_lse, query_first, row_count)
        delta_rows = lax.dynamic_slice_in_dim(all_delta, query_first, row_count)
        query_docs = lax.dynamic_slice_in_dim(doc_ids, query_first, row_count)
        scores, allowed = score_pair(query_block, own_keys, query_docs, own_docs)
        weights = jnp.where(allowed, jnp.exp(scores - lse_rows[..., None]), 0.0)
        d_value_sum = d_value_sum + jnp.einsum(
            "qhk,qhd->khd",
            weights.astype(jnp.bfloat16),
            grad_block,
            preferred_element_type=jnp.float32,
        )
        d_weights = jnp.einsum(
            "qhd,khd->qhk", grad_block, own_values, preferred_element_type=jnp.float32
        )
        d_scores = (weights * (d_weights - delta_rows[..., None])).astype(jnp.bfloat16)
        d_key_sum = d_key_sum + jnp.einsum(
            "qhk,qhd->khd", d_scores, query_block, preferred_element_type=jnp.float32
        )
        return (d_key_sum, d_value_sum)

    def key_grad_fold(carry_now, portion, offset):
        return over_blocks(carry_now, portion, offset, seq_lower, seq_upper, key_grad_step)

    query_grads = jnp.stack([regrouped[0], d_heads.reshape(group_rows, inner_width)])
    zero_keys = jnp.zeros((group_rows, heads_dev, HEAD_DIM), jnp.float32)
    d_keys, d_values = fold_peers(query_grads, key_grad_fold, (zero_keys, zero_keys))
    d_keys = d_keys * score_scale
    back_grads = jnp.stack(
        [
            d_queries.reshape(group_rows, inner_width),
            d_keys.reshape(group_rows, inner_width),
            d_values.reshape(group_rows, inner_width),
        ]
    ).astype(jnp.bfloat16)
    back_grads = back_grads.reshape(3, group_rows, 1, inner_width)
    token_grads = lax.all_to_all(
        back_grads, "seq", split_axis=1, concat_axis=2, tiled=True
    ).reshape(3, tok_rows, model_width)
    d_turned_q = token_grads[0].astype(jnp.float32).reshape(tok_rows, HEADS, HEAD_DIM)
    d_turned_k = token_grads[1].astype(jnp.float32).reshape(tok_rows, HEADS, HEAD_DIM)
    d_raw_q, d_raw_k = unturn((d_turned_q, d_turned_k))
    d_projected = jnp.concatenate(
        [
            d_raw_q.reshape(tok_rows, model_width).astype(jnp.bfloat16),
            d_raw_k.reshape(tok_rows, model_width).astype(jnp.bfloat16),
            token_grads[2],
        ],
        axis=1,
    )
    grad_qkv = left_product(layer_input, d_projected)
    d_input = d_first + right_product(d_projected, qkv_full)
    shards = (
        lax.psum_scatter(
            grad_qkv.astype(jnp.bfloat16), "fsdp", scatter_dimension=0, tiled=True
        ).astype(jnp.float32),
        lax.psum_scatter(
            grad_out.astype(jnp.bfloat16), "fsdp", scatter_dimension=0, tiled=True
        ).astype(jnp.float32),
        lax.psum_scatter(
            grad_gain_one.astype(jnp.bfloat16), "fsdp", scatter_dimension=0, tiled=True
        ).astype(jnp.float32),
        lax.psum_scatter(
            grad_bias_one.astype(jnp.bfloat16), "fsdp", scatter_dimension=0, tiled=True
        ).astype(jnp.float32),
        lax.psum_scatter(
            grad_up.astype(jnp.bfloat16), "fsdp", scatter_dimension=0, tiled=True
        ).astype(jnp.float32),
        lax.psum_scatter(
            grad_gate.astype(jnp.bfloat16), "fsdp", scatter_dimension=0, tiled=True
        ).astype(jnp.float32),
        lax.psum_scatter(
            grad_down.astype(jnp.bfloat16), "fsdp", scatter_dimension=0, tiled=True
        ).astype(jnp.float32),
        lax.psum_scatter(
            grad_gain_two.astype(jnp.bfloat16), "fsdp", scatter_dimension=0, tiled=True
        ).astype(jnp.float32),
        lax.psum_scatter(
            grad_bias_two.astype(jnp.bfloat16), "fsdp", scatter_dimension=0, tiled=True
        ).astype(jnp.float32),
    )
    (
        part_qkv,
        part_out,
        part_gain_one,
        part_bias_one,
        part_up,
        part_gate,
        part_down,
        part_gain_two,
        part_bias_two,
    ) = shards
    summed = (
        lax.psum(part_qkv.astype(jnp.bfloat16), "seq").astype(jnp.float32),
        lax.psum(part_out.astype(jnp.bfloat16), "seq").astype(jnp.float32),
        lax.psum(part_gain_one.astype(jnp.bfloat16), "seq").astype(jnp.float32),
        lax.psum(part_bias_one.astype(jnp.bfloat16), "seq").astype(jnp.float32),
        lax.psum(part_up.astype(jnp.bfloat16), "seq").astype(jnp.float32),
        lax.psum(part_gate.astype(jnp.bfloat16), "seq").astype(jnp.float32),
        lax.psum(part_down.astype(jnp.bfloat16), "seq").astype(jnp.float32),
        lax.psum(part_gain_two.astype(jnp.bfloat16), "seq").astype(jnp.float32),
        lax.psum(part_bias_two.astype(jnp.bfloat16), "seq").astype(jnp.float32),
    )
    return (
        result.astype(jnp.bfloat16),
        d_input.astype(jnp.bfloat16),
        summed[0],
        summed[1],
        summed[2],
        summed[3],
        summed[4],
        summed[5],
        summed[6],
        summed[7],
        summed[8],
    )


def solution(mesh):
    in_specs = (
        P(("fsdp", "seq"), None),
        P(("fsdp", "seq"), None),
        P(),
        P("fsdp", None),
        P("fsdp", None),
        P("fsdp"),
        P("fsdp"),
        P("fsdp", None),
        P("fsdp", None),
        P("fsdp", None),
        P("fsdp"),
        P("fsdp"),
    )
    out_specs = (
        P(("fsdp", "seq"), None),
        P(("fsdp", "seq"), None),
        P("fsdp", None),
        P("fsdp", None),
        P("fsdp"),
        P("fsdp"),
        P("fsdp", None),
        P("fsdp", None),
        P("fsdp", None),
        P("fsdp"),
        P("fsdp"),
    )
    return jax.shard_map(local, mesh=mesh, in_specs=in_specs, out_specs=out_specs, check_vma=False)
```

profile of v0, /device:TPU:0, one launch (start us, length us, event | category | flops | bytes accessed | tf_op | source)
XLA Modules:
  0.0 1811.6 jit_solution(15487966037198221241)
XLA Ops:
  14.6 64.1 %all-gather.6.cloned.1.call-done = bf16[768,2304]{1,0:T(8,128)(2,1)} async-done(((bf16[96,2304]{1,0:T(8,128)(2,1)}), bf16[768,2304]{1,0:T(8,128)(2,1)}) %all-gather.6.cloned.1.call-update) | async-done | bytes 3538960 | tf_op jit(solution)/shard_map/all_gather | solution.py:123
  83.2 18.4 %all_to_all.60 = bf16[3,256,4,192]{1,3,0,2:T(8,128)(2,1)S(1)} all-to-all(bf16[3,256,4,192]{1,3,0,2:T(8,128)(2,1)S(1)} %copy.163), channel_id=1, replica_groups=mesh['fsdp'=8,'seq'=4] {'seq'}, dimensions={2} | all-to-all | bytes 2359296 | tf_op jit(solution)/shard_map/all_to_all | solution.py:178
  106.8 22.4 %collective-permute-done = bf16[2,1024,192]{1,2,0:T(8,128)(2,1)S(1)} collective-permute-done((bf16[2,1024,192]{1,2,0:T(8,128)(2,1)S(1)}, bf16[2,1024,192]{1,2,0:T(8,128)(2,1)S(1)}, u32[]{:S(2)}, u32[]{:S(2)}) %collective-permute-start) | collective-permute-done | bytes 786464 | tf_op jit(solution)/shard_map/ppermute | solution.py:21
  132.2 53.4 %collective-permute-done.1 = bf16[2,2048,192]{1,2,0:T(8,128)(2,1)} collective-permute-done((bf16[2,2048,192]{1,2,0:T(8,128)(2,1)}, bf16[2,2048,192]{1,2,0:T(8,128)(2,1)}, u32[]{:S(2)}, u32[]{:S(2)}) %collective-permute-start.1) | collective-permute-done | bytes 1572896 | tf_op jit(solution)/shard_map/ppermute | solution.py:21
  218.9 26.5 %while.194 = (s32[]{:T(128)}, f32[1024,3]{0,1:T(4,128)S(1)}, f32[1024,3]{0,1:T(4,128)S(1)}, f32[1024,3,64]{0,2,1:T(8,128)S(1)}, s32[]{:T(128)}, /*index=5*/s32[]...) while((s32[]{:T(128)}, f32[1024,3]{0,1:T(4,128)S(1)}, ...), condition=%wide.region_17.18_spmd, body=%wide.region_12.17_spmd.sunk | while | flops 424024064 | bytes 24324504 | solution.py:85
  245.4 132.7 %collective-permute-done.2 = bf16[2,4096,192]{1,2,0:T(8,128)(2,1)} collective-permute-done((bf16[2,4096,192]{1,2,0:T(8,128)(2,1)}, bf16[2,4096,192]{1,2,0:T(8,128)(2,1)}, u32[]{:S(2)}, u32[]{:S(2)}) %collective-permute-start.2) | collective-permute-done | bytes 3145760 | tf_op jit(solution)/shard_map/ppermute | solution.py:21
  378.1 53.1 %while.195 = (s32[]{:T(128)}, f32[1024,3]{0,1:T(4,128)S(1)}, f32[1024,3]{0,1:T(4,128)S(1)}, f32[1024,3,64]{0,2,1:T(8,128)S(1)}, s32[]{:T(128)}, /*index=5*/s32[]...) while((s32[]{:T(128)}, f32[1024,3]{0,1:T(4,128)S(1)}, ...), condition=%wide.region_23.24_spmd, body=%wide.region_18.23_spmd.sunk | while | flops 424024064 | bytes 24324504 | solution.py:85
  440.4 28.3 %all-reduce.13 = (bf16[768]{0:T(1024)(128)(2,1)S(1)}, bf16[768]{0:T(1024)(128)(2,1)S(1)}, bf16[768]{0:T(1024)(128)(2,1)S(1)}) all-reduce(bf16[768]{0:T(1024)(128)(2,1)S(1)} %dynamic-update-slice.1, bf16[768]{0:T(1024)(128)(2,1)S(1)} %dynamic-update-slice, ...), channel_id=1, replica_groups=mesh['fsdp'=8,'seq'=4] {'fsdp'}, use_global_device_ids=true, to_apply=%add.5 | all-reduce | flops 2304 | bytes 9216
  489.8 16.3 all-gather.14.cloned.1.call-done
  540.3 18.5 %collective-permute-done.3 = bf16[2,1024,192]{1,2,0:T(8,128)(2,1)S(1)} collective-permute-done((bf16[2,1024,192]{1,2,0:T(8,128)(2,1)S(1)}, bf16[2,1024,192]{1,2,0:T(8,128)(2,1)S(1)}, u32[]{:S(2)}, u32[]{:S(2)}) %collective-permute-start.3) | collective-permute-done | bytes 786464 | tf_op jit(solution)/shard_map/ppermute | solution.py:21
  560.0 34.5 %collective-permute-done.4 = bf16[2,2048,192]{1,2,0:T(8,128)(2,1)S(1)} collective-permute-done((bf16[2,2048,192]{1,2,0:T(8,128)(2,1)S(1)}, bf16[2,2048,192]{1,2,0:T(8,128)(2,1)S(1)}, u32[]{:S(2)}, u32[]{:S(2)}) %collective-permute-start.4) | collective-permute-done | bytes 1572896 | tf_op jit(solution)/shard_map/ppermute | solution.py:21
  606.9 148.8 %all_gather.42 = f32[8192,3]{0,1:T(4,128)} all-gather(f32[1024,3]{0,1:T(4,128)S(1)} %log_add_fusion), channel_id=1, replica_groups=mesh['fsdp'=8,'seq'=4] {'fsdp'}, dimensions={0}, use_global_device_ids=true | all-gather | bytes 110592 | tf_op jit(solution)/shard_map/all_gather | solution.py:264
  759.8 21.4 %while.196 = (s32[]{:T(128)}, f32[1024,3,64]{0,2,1:T(8,128)}, s32[]{:T(128)}, s32[]{:T(128)}, s32[]{:T(128)}, /*index=5*/s32[1024]{0:T(1024)S(1)}, s32[8192]{0:T...) while((s32[]{:T(128)}, f32[1024,3,64]{0,2,1:T(8,128)}, ...), condition=%wide.region_36.37_spmd, body=%wide.region_33.36_spmd.sunk | while | flops 614137856 | bytes 17402232 | solution.py:85
  781.2 21.4 %while.197 = (s32[]{:T(128)}, f32[1024,3,64]{0,2,1:T(8,128)}, s32[]{:T(128)}, s32[]{:T(128)}, s32[]{:T(128)}, /*index=5*/s32[1024]{0:T(1024)S(1)}, s32[8192]{0:T...) while((s32[]{:T(128)}, f32[1024,3,64]{0,2,1:T(8,128)}, ...), condition=%wide.region_40.41_spmd, body=%wide.region_37.40_spmd.sunk | while | flops 614137856 | bytes 17402232 | solution.py:85
  802.6 31.0 %all_gather.43 = f32[8192,3]{0,1:T(4,128)S(1)} all-gather(f32[1024,3]{0,1:T(4,128)S(1)} %get-tuple-element.5854), channel_id=1, replica_groups=mesh['fsdp'=8,'seq'=4] {'fsdp'}, dimensions={0}, use_global_device_ids=true | all-gather | bytes 110592 | tf_op jit(solution)/shard_map/all_gather | solution.py:265
  834.6 31.9 %while.200 = (s32[]{:T(128)}, f32[1024,3,64]{0,2,1:T(8,128)S(1)}, f32[1024,3,64]{0,2,1:T(8,128)}, s32[]{:T(128)}, s32[]{:T(128)}, /*index=5*/s32[]{:T(128)}, s32...) while((s32[]{:T(128)}, f32[1024,3,64]{0,2,1:T(8,128)S(1)}, ...), condition=%wide.region_52.53_spmd, body=%wide.region_49.52_spmd.sunk | while | flops 821952512 | bytes 26005932 | solution.py:85
  834.6 16.0 conditional.32
  850.6 16.0 conditional.32
  867.5 46.7 %while.198 = (s32[]{:T(128)}, f32[1024,3,64]{0,2,1:T(8,128)}, s32[]{:T(128)}, s32[]{:T(128)}, s32[]{:T(128)}, /*index=5*/s32[1024]{0:T(1024)S(1)}, s32[8192]{0:T...) while((s32[]{:T(128)}, f32[1024,3,64]{0,2,1:T(8,128)}, ...), condition=%wide.region_44.45_spmd, body=%wide.region_41.44_spmd.sunk | while | flops 614137856 | bytes 19024304 | solution.py:85
  914.1 94.4 %while.199 = (s32[]{:T(128)}, f32[1024,3,64]{0,2,1:T(8,128)}, s32[]{:T(128)}, s32[]{:T(128)}, s32[]{:T(128)}, /*index=5*/s32[1024]{0:T(1024)S(1)}, s32[8192]{0:T...) while((s32[]{:T(128)}, f32[1024,3,64]{0,2,1:T(8,128)}, ...), condition=%wide.region_48.49_spmd, body=%wide.region_45.48_spmd.sunk | while | flops 614137856 | bytes 17451412 | solution.py:85
  914.3 11.9 conditional.31
  973.2 11.8 conditional.31
  996.7 11.8 conditional.31
  1009.7 32.1 %while.201 = (s32[]{:T(128)}, f32[1024,3,64]{0,2,1:T(8,128)S(1)}, f32[1024,3,64]{0,2,1:T(8,128)}, s32[]{:T(128)}, s32[]{:T(128)}, /*index=5*/s32[]{:T(128)}, s32...) while((s32[]{:T(128)}, f32[1024,3,64]{0,2,1:T(8,128)S(1)}, ...), condition=%wide.region_56.57_spmd, body=%wide.region_53.56_spmd.sunk | while | flops 821952512 | bytes 26005932 | solution.py:85
  1009.7 16.0 conditional.33
  1025.7 16.0 conditional.33
  1041.7 68.0 %while.202 = (s32[]{:T(128)}, f32[1024,3,64]{0,2,1:T(8,128)S(1)}, f32[1024,3,64]{0,2,1:T(8,128)}, s32[]{:T(128)}, s32[]{:T(128)}, /*index=5*/s32[]{:T(128)}, s32...) while((s32[]{:T(128)}, f32[1024,3,64]{0,2,1:T(8,128)S(1)}, ...), condition=%wide.region_60.61_spmd, body=%wide.region_57.60_spmd.sunk | while | flops 821952512 | bytes 27578824 | solution.py:85
  1042.0 17.0 conditional.34
  1058.9 16.9 conditional.34
  1075.8 16.9 conditional.34
  1092.8 16.9 conditional.34
  1109.7 135.4 %while.203 = (s32[]{:T(128)}, f32[1024,3,64]{0,2,1:T(8,128)S(1)}, f32[1024,3,64]{0,2,1:T(8,128)}, s32[]{:T(128)}, s32[]{:T(128)}, /*index=5*/s32[]{:T(128)}, s32...) while((s32[]{:T(128)}, f32[1024,3,64]{0,2,1:T(8,128)S(1)}, ...), condition=%wide.region_64.65_spmd, body=%wide.region_61.64_spmd.sunk | while | flops 821952512 | bytes 27578824 | solution.py:85
  1109.7 16.9 conditional.35
  1126.6 16.9 conditional.35
  1143.6 16.9 conditional.35
  1160.5 16.9 conditional.35
  1177.4 16.9 conditional.35
  1194.3 16.9 conditional.35
  1211.3 16.9 conditional.35
  1228.2 16.9 conditional.35
  1250.4 29.2 %all_to_all.61 = bf16[3,1024,1,192]{3,0,2,1:T(4,128)(2,1)} all-to-all(bf16[3,1024,1,192]{3,0,2,1:T(4,128)(2,1)S(1)} %copy.175), channel_id=1, replica_groups=mesh['fsdp'=8,'seq'=4] {'seq'}, dimensions={1} | all-to-all | bytes 2359296 | tf_op jit(solution)/shard_map/all_to_all | solution.py:332
  1308.3 62.8 %reduce-scatter.16.cloned.1.call-done = bf16[96,2304]{1,0:T(8,128)(2,1)} async-done(((bf16[768,2304]{1,0:T(8,128)(2,1)}), bf16[96,2304]{1,0:T(8,128)(2,1)}) %reduce-scatter.16.cloned.1.call-update) | async-done | bytes 442384
  1373.1 65.5 %reduce-scatter.8.cloned.1.call-done = bf16[96,768]{1,0:T(8,128)(2,1)} async-done(((bf16[768,768]{1,0:T(8,128)(2,1)}), bf16[96,768]{1,0:T(8,128)(2,1)}) %reduce-scatter.8.cloned.1.call-update) | async-done | bytes 147472 | tf_op jit(solution)/shard_map/reduce_scatter | solution.py:352
  1438.6 98.1 %reduce-scatter.14.cloned.1.call-done = bf16[384,768]{1,0:T(8,128)(2,1)} async-done(((bf16[3072,768]{1,0:T(8,128)(2,1)}), bf16[384,768]{1,0:T(8,128)(2,1)}) %reduce-scatter.14.cloned.1.call-update) | async-done | bytes 589840 | tf_op jit(solution)/shard_map/reduce_scatter | solution.py:367
  1536.7 98.7 %reduce-scatter.10.cloned.1.call-done = bf16[96,3072]{1,0:T(8,128)(2,1)} async-done(((bf16[768,3072]{1,0:T(8,128)(2,1)}), bf16[96,3072]{1,0:T(8,128)(2,1)}) %reduce-scatter.10.cloned.1.call-update) | async-done | bytes 589840 | tf_op jit(solution)/shard_map/reduce_scatter | solution.py:361
  1635.4 98.5 %reduce-scatter.12.cloned.1.call-done = bf16[96,3072]{1,0:T(8,128)(2,1)} async-done(((bf16[768,3072]{1,0:T(8,128)(2,1)}), bf16[96,3072]{1,0:T(8,128)(2,1)}) %reduce-scatter.12.cloned.1.call-update) | async-done | bytes 589840 | tf_op jit(solution)/shard_map/reduce_scatter | solution.py:364
  1735.0 35.9 %all-reduce.12 = (bf16[768]{0:T(1024)(128)(2,1)S(1)}, bf16[768]{0:T(1024)(128)(2,1)S(1)}, bf16[768]{0:T(1024)(128)(2,1)S(1)}, bf16[768]{0:T(1024)(128)(2,1)S(1)}, bf16[768]{0:T(1024)(128)(2,1)S(1)}) all-reduce(bf16[768]{0:T(1024)(128)(2,1)S(1)} %dynamic-update-slice.3, ...), channel_id=1, replica_groups=mesh['fsdp'=8,'seq'=4] {'fsdp'}, use_global_device_ids=true, to_apply=%add.7 | all-reduce | flops 3840 | bytes 15360
  1784.3 11.9 all-reduce.18.cloned.1.call-done
  (739 shorter events, 994.8 us)
Async XLA Ops:
  7.2 71.5 %copy-start.30 = (bf16[256,768]{1,0:T(8,128)(2,1)S(1)}, bf16[256,768]{1,0:T(8,128)(2,1)}, u32[]{:S(2)}) copy-start(bf16[256,768]{1,0:T(8,128)(2,1)} %param.60) | copy-start | bytes 1179652
  7.2 71.5 %all-gather.6.cloned.1.call-start = ((), (), s32[]{:S(2)}) async-start(), calls=%async_computation.9 | async-start | bytes 3981312 | tf_op jit(solution)/shard_map/all_gather | solution.py:123
  9.4 464.9 %all-gather.8.cloned.1.call-start = ((), (), s32[]{:S(2)}) async-start(), calls=%async_computation.10 | async-start | bytes 1327104 | tf_op jit(solution)/shard_map/all_gather | solution.py:124
  11.1 465.8 %all-gather.10.cloned.1.call-start = ((), (), s32[]{:S(2)}) async-start(), calls=%async_computation.11 | async-start | bytes 5308416 | tf_op jit(solution)/shard_map/all_gather | solution.py:128
  13.3 469.2 %all-gather.12.cloned.1.call-start = ((), (), s32[]{:S(2)}) async-start(), calls=%async_computation.12 | async-start | bytes 5308416 | tf_op jit(solution)/shard_map/all_gather | solution.py:127
  14.3 491.8 %all-gather.14.cloned.1.call-start = ((), (), s32[]{:S(2)}) async-start(), calls=%async_computation.13 | async-start | bytes 5308416 | tf_op jit(solution)/shard_map/all_gather | solution.py:129
  14.6 68.1 %copy-start.45 = (f32[256,32]{0,1:T(8,128)}, f32[256,32]{0,1:T(8,128)S(1)}, u32[]{:S(2)}) copy-start(f32[256,32]{0,1:T(8,128)S(1)} %get-tuple-element.4241) | copy-start | bytes 98308
  14.6 68.1 %copy-start.47 = (f32[256,32]{0,1:T(8,128)}, f32[256,32]{0,1:T(8,128)S(1)}, u32[]{:S(2)}) copy-start(f32[256,32]{0,1:T(8,128)S(1)} %get-tuple-element.4242) | copy-start | bytes 98308
  103.9 25.3 %collective-permute-start = (bf16[2,1024,192]{1,2,0:T(8,128)(2,1)S(1)}, bf16[2,1024,192]{1,2,0:T(8,128)(2,1)S(1)}, u32[]{:S(2)}, u32[]{:S(2)}) collective-permute-start(bf16[2,1024,192]{1,2,0:T(8,128)(2,1)S(1)} %slice.183), channel_id=1, source_target_pairs={{0,4},{4,0},{8,12},{12,8},{16,20},{20,16},{24,28},{28,24},{1,5},{5... | collective-permute-start | bytes 2359304 | tf_op jit(solution)/shard_map/ppermute | solution.py:21
  106.7 85.3 %copy-start.36 = (s32[8192]{0:T(1024)S(1)}, s32[8192]{0:T(1024)}, u32[]{:S(2)}) copy-start(s32[8192]{0:T(1024)} %param.62) | copy-start | bytes 98308
  131.0 54.7 %collective-permute-start.1 = (bf16[2,2048,192]{1,2,0:T(8,128)(2,1)}, bf16[2,2048,192]{1,2,0:T(8,128)(2,1)}, u32[]{:S(2)}, u32[]{:S(2)}) collective-permute-start(bf16[2,2048,192]{1,2,0:T(8,128)(2,1)} %maximum_select_fusion.2), channel_id=1, source_target_pairs={{0,8},{4,12},{8,0},{12,4},{16,24},{20,28},{24,16},{28,20},{1,9},{5... | collective-permute-start | bytes 4718600 | tf_op jit(solution)/shard_map/ppermute | solution.py:21
  190.8 187.3 %collective-permute-start.2 = (bf16[2,4096,192]{1,2,0:T(8,128)(2,1)}, bf16[2,4096,192]{1,2,0:T(8,128)(2,1)}, u32[]{:S(2)}, u32[]{:S(2)}) collective-permute-start(bf16[2,4096,192]{1,2,0:T(8,128)(2,1)} %maximum_select_fusion), channel_id=1, source_target_pairs={{0,16},{4,20},{8,24},{12,28},{16,0},{20,4},{24,8},{28,12},{1,17},{... | collective-permute-start | bytes 9437192 | tf_op jit(solution)/shard_map/ppermute | solution.py:21
  378.1 60.4 %copy-start.68 = (f32[96]{0:T(128)S(1)}, f32[96]{0:T(128)}, u32[]{:S(2)}) copy-start(f32[96]{0:T(128)} %param.65) | copy-start | bytes 1156
  378.1 60.4 %copy-start.69 = (f32[96]{0:T(128)S(1)}, f32[96]{0:T(128)}, u32[]{:S(2)}) copy-start(f32[96]{0:T(128)} %param.66) | copy-start | bytes 1156
  378.1 60.4 %copy-start.70 = (f32[96]{0:T(128)S(1)}, f32[96]{0:T(128)}, u32[]{:S(2)}) copy-start(f32[96]{0:T(128)} %param.70) | copy-start | bytes 1156
  378.1 60.4 %copy-start.66 = (u32[32]{0:T(128)S(1)}, u32[32]{0:T(128)}, u32[]{:S(2)}) copy-start(u32[32]{0:T(128)} %constant.719) | copy-start | bytes 388
  434.3 34.4 %all-to-all-start.1 = ((bf16[4,2,24576]{2,1,0:T(2,128)(2,1)}), bf16[4,2,24576]{2,1,0:T(2,128)(2,1)}, u32[]{:S(2)}, u32[]{:S(2)}) async-start(bf16[4,2,24576]{2,1,0:T(2,128)(2,1)} %reshape.619), calls=%async_computation.1 | async-start | bytes 786432 | tf_op jit(solution)/shard_map/all_to_all | solution.py:228
  468.7 43.0 %copy-start.50 = (f32[768]{0:T(1024)}, f32[768]{0:T(1024)S(1)}, u32[]{:S(2)}) copy-start(f32[768]{0:T(1024)S(1)} %convert_element_type.398) | copy-start | bytes 9220
  522.4 37.0 %copy-start.59 = (f32[256]{0:T(256)}, f32[256]{0:T(256)S(1)}, u32[]{:S(2)}) copy-start(f32[256]{0:T(256)S(1)} %negate_multiply_fusion) | copy-start | bytes 3076
  524.7 11.6 all-to-all-start.2
  528.8 842.3 %reduce-scatter.16.cloned.1.call-start = ((), (), s32[]{:S(2)}) async-start(), calls=%async_computation.18 | async-start | bytes 3981312
  537.6 21.2 %copy-start.17 = (bf16[4,256,1,192]{1,0,3,2:T(4,128)(2,1)}, bf16[4,256,1,192]{1,0,3,2:T(4,128)(2,1)S(1)}, u32[]{:S(2)}) copy-start(bf16[4,256,1,192]{1,0,3,2:T(4,128)(2,1)S(1)} %copy.170) | copy-start | bytes 1179652
  539.7 19.1 %collective-permute-start.3 = (bf16[2,1024,192]{1,2,0:T(8,128)(2,1)S(1)}, bf16[2,1024,192]{1,2,0:T(8,128)(2,1)S(1)}, u32[]{:S(2)}, u32[]{:S(2)}) collective-permute-start(bf16[2,1024,192]{1,2,0:T(8,128)(2,1)S(1)} %constant_dynamic-update-slice_fusion), channel_id=1, source_target_pairs={{0,4},{4,0},{8,12},{12,8},{16,20},{20,16},{24,28},{28,24},{1,5},{5... | collective-permute-start | bytes 2359304 | tf_op jit(solution)/shard_map/ppermute | solution.py:21
  558.8 39.3 %copy-start.6 = (bf16[2,1024,192]{1,2,0:T(8,128)(2,1)}, bf16[2,1024,192]{1,2,0:T(8,128)(2,1)S(1)}, u32[]{:S(2)}) copy-start(bf16[2,1024,192]{1,2,0:T(8,128)(2,1)S(1)} %collective-permute-done.3) | copy-start | bytes 2359300
  559.4 200.4 %copy-start.1 = (bf16[2,1024,192]{1,2,0:T(8,128)(2,1)S(1)}, bf16[2,1024,192]{1,2,0:T(8,128)(2,1)}, u32[]{:S(2)}) copy-start(bf16[2,1024,192]{1,2,0:T(8,128)(2,1)} %copy-done) | copy-start | bytes 2359300
  559.4 35.1 %collective-permute-start.4 = (bf16[2,2048,192]{1,2,0:T(8,128)(2,1)S(1)}, bf16[2,2048,192]{1,2,0:T(8,128)(2,1)S(1)}, u32[]{:S(2)}, u32[]{:S(2)}) collective-permute-start(bf16[2,2048,192]{1,2,0:T(8,128)(2,1)S(1)} %maximum_select_fusion.3), channel_id=1, source_target_pairs={{0,8},{4,12},{8,0},{12,4},{16,24},{20,28},{24,16},{28,20},{1,9},{5... | collective-permute-start | bytes 4718600 | tf_op jit(solution)/shard_map/ppermute | solution.py:21
  598.1 511.6 %collective-permute-start.5 = (bf16[2,4096,192]{1,2,0:T(8,128)(2,1)}, bf16[2,4096,192]{1,2,0:T(8,128)(2,1)}, u32[]{:S(2)}, u32[]{:S(2)}) collective-permute-start(bf16[2,4096,192]{1,2,0:T(8,128)(2,1)} %maximum_select_fusion.1), channel_id=1, source_target_pairs={{0,16},{4,20},{8,24},{12,28},{16,0},{20,4},{24,8},{28,12},{1,17},{... | collective-permute-start | bytes 9437192 | tf_op jit(solution)/shard_map/ppermute | solution.py:21
  781.2 53.4 %copy-start.5 = (bf16[2,1024,192]{1,2,0:T(8,128)(2,1)S(1)}, bf16[2,1024,192]{1,2,0:T(8,128)(2,1)}, u32[]{:S(2)}) copy-start(bf16[2,1024,192]{1,2,0:T(8,128)(2,1)} %copy-done.4) | copy-start | bytes 2359300
  802.6 32.0 %copy-start.52 = (f32[1024,3]{0,1:T(4,128)}, f32[1024,3]{0,1:T(4,128)S(1)}, u32[]{:S(2)}) copy-start(f32[1024,3]{0,1:T(4,128)S(1)} %get-tuple-element.5857) | copy-start | bytes 36868
  914.1 95.6 %copy-start.7 = (bf16[2,1024,192]{1,2,0:T(8,128)(2,1)S(1)}, bf16[2,1024,192]{1,2,0:T(8,128)(2,1)}, u32[]{:S(2)}) copy-start(bf16[2,1024,192]{1,2,0:T(8,128)(2,1)} %copy-done.6) | copy-start | bytes 2359300
  914.1 95.6 %copy-start.24 = (f32[1024,3,64]{0,2,1:T(8,128)S(1)}, f32[1024,3,64]{0,2,1:T(8,128)}, u32[]{:S(2)}) copy-start(f32[1024,3,64]{0,2,1:T(8,128)} %copy-done.23) | copy-start | bytes 2359300
  1292.8 145.8 %reduce-scatter.8.cloned.1.call-start = ((), (), s32[]{:S(2)}) async-start(), calls=%async_computation.14 | async-start | bytes 1327104 | tf_op jit(solution)/shard_map/reduce_scatter | solution.py:352
  1294.5 242.3 %reduce-scatter.14.cloned.1.call-start = ((), (), s32[]{:S(2)}) async-start(), calls=%async_computation.17 | async-start | bytes 5308416 | tf_op jit(solution)/shard_map/reduce_scatter | solution.py:367
  1298.3 337.2 %reduce-scatter.10.cloned.1.call-start = ((), (), s32[]{:S(2)}) async-start(), calls=%async_computation.15 | async-start | bytes 5308416 | tf_op jit(solution)/shard_map/reduce_scatter | solution.py:361
  1304.4 429.5 %reduce-scatter.12.cloned.1.call-start = ((), (), s32[]{:S(2)}) async-start(), calls=%async_computation.16 | async-start | bytes 5308416 | tf_op jit(solution)/shard_map/reduce_scatter | solution.py:364
  1308.1 425.9 %copy-start.71 = (f32[96]{0:T(128)S(1)}, f32[96]{0:T(128)}, u32[]{:S(2)}) copy-start(f32[96]{0:T(128)} %param.71) | copy-start | bytes 1156
  1308.1 425.9 %copy-start.21 = (bf16[256,768]{1,0:T(8,128)(2,1)S(1)}, bf16[256,768]{1,0:T(8,128)(2,1)}, u32[]{:S(2)}) copy-start(bf16[256,768]{1,0:T(8,128)(2,1)} %param.61) | copy-start | bytes 1179652
  1308.1 426.9 %copy-start.61 = (bf16[768]{0:T(1024)(128)(2,1)S(1)}, bf16[768]{0:T(1024)(128)(2,1)}, u32[]{:S(2)}) copy-start(bf16[768]{0:T(1024)(128)(2,1)} %get-tuple-element.3859) | copy-start | bytes 4612
  1308.1 426.9 %copy-start.64 = (bf16[768]{0:T(1024)(128)(2,1)S(1)}, bf16[768]{0:T(1024)(128)(2,1)}, u32[]{:S(2)}) copy-start(bf16[768]{0:T(1024)(128)(2,1)} %get-tuple-element.3857) | copy-start | bytes 4612
  1308.1 426.9 %copy-start.65 = (bf16[768]{0:T(1024)(128)(2,1)S(1)}, bf16[768]{0:T(1024)(128)(2,1)}, u32[]{:S(2)}) copy-start(bf16[768]{0:T(1024)(128)(2,1)} %get-tuple-element.3861) | copy-start | bytes 4612
  1308.1 471.3 %copy-start.3 = (f32[256,768]{1,0:T(8,128)S(1)}, f32[256,768]{1,0:T(8,128)}, u32[]{:S(2)}) copy-start(f32[256,768]{1,0:T(8,128)} %copy-done.2) | copy-start | bytes 2359300
  1308.1 471.3 %copy-start.51 = (f32[768]{0:T(1024)S(1)}, f32[768]{0:T(1024)}, u32[]{:S(2)}) copy-start(f32[768]{0:T(1024)} %copy-done.50) | copy-start | bytes 9220
  1308.1 471.3 %copy-start.56 = (f32[256]{0:T(256)S(1)}, f32[256]{0:T(256)}, u32[]{:S(2)}) copy-start(f32[256]{0:T(256)} %copy-done.55) | copy-start | bytes 3076
  1308.1 471.3 %copy-start.58 = (f32[256]{0:T(256)S(1)}, f32[256]{0:T(256)}, u32[]{:S(2)}) copy-start(f32[256]{0:T(256)} %copy-done.57) | copy-start | bytes 3076
  1308.2 472.2 %copy-start.38 = (bf16[1,256,4,1,192]{1,4,3,2,0:T(8,128)(2,1)S(1)}, bf16[1,256,4,1,192]{1,4,3,2,0:T(8,128)(2,1)}, u32[]{:S(2)}) copy-start(bf16[1,256,4,1,192]{1,4,3,2,0:T(8,128)(2,1)} %copy-done.37) | copy-start | bytes 1179652
  1308.2 472.2 %copy-start.42 = (bf16[256,12,64]{0,2,1:T(8,128)(2,1)S(1)}, bf16[256,12,64]{0,2,1:T(8,128)(2,1)}, u32[]{:S(2)}) copy-start(bf16[256,12,64]{0,2,1:T(8,128)(2,1)} %copy-done.41) | copy-start | bytes 1179652
  1308.2 472.2 %copy-start.44 = (bf16[256,12,64]{0,2,1:T(8,128)(2,1)S(1)}, bf16[256,12,64]{0,2,1:T(8,128)(2,1)}, u32[]{:S(2)}) copy-start(bf16[256,12,64]{0,2,1:T(8,128)(2,1)} %copy-done.43) | copy-start | bytes 1179652
  1308.2 488.0 %all-reduce.18.cloned.1.call-start = ((), (), s32[]{:S(2)}) async-start(), calls=%async_computation.19 | async-start | bytes 5013504 | tf_op jit(solution)/shard_map/psum | solution.py:389
  (72 other events, 330.5 us)
Sparse Core Ops, SparseCore 0:
  10.8 67.8 all-gather.5
  81.5 45.1 all-gather.7
  129.4 178.4 all-gather.9
  310.5 114.6 all-gather.11
  427.8 78.2 all-gather.13
  1292.9 78.1 reduce-scatter.15
  1375.0 63.5 reduce-scatter.7
  1442.3 94.4 reduce-scatter.13
  1540.4 95.0 reduce-scatter.9
  1638.9 94.9 reduce-scatter.11
  1737.3 58.8 all-reduce.17
where the time goes:
time: 1820 us; the launch traced here: 1810 us
  waiting for transfers between devices  783 us (43%)
  matrix products  502 us (28%)
  blocking collectives  298 us (16%)
  local copies, waits for them, and re-layouts  112 us (6%)
  other arithmetic  81.8 us (4%)
    ppermute x6, waiting for transfers between devices, swapped(): return lax.ppermute(value, axis, pairs)  262 us
    all_gather x1, blocking collectives, local(): lax.all_gather(log_total, 'fsdp', axis=0, tiled=True)  149 us
    dot_general x48, matrix products, score_pair(): jnp.einsum('qhd,khd->qhk', query_block, key_block, preferred_element_type...  137 us
    dot_general x16, matrix products, query_grad_step(): jnp.einsum('qhk,khd->qhd', d_scores, key_block, preferred_element_type=jn...  105 us
    reduce_scatter x1, waiting for transfers between devices, local(): lax.psum_scatter(grad_up.astype(jnp.bfloat16), 'fsdp', scatter_dimension=...  98.7 us
    reduce_scatter x1, waiting for transfers between devices, local(): lax.psum_scatter(grad_gate.astype(jnp.bfloat16), 'fsdp', scatter_dimensio...  98.5 us
    reduce_scatter x1, waiting for transfers between devices, local(): lax.psum_scatter(grad_down.astype(jnp.bfloat16), 'fsdp', scatter_dimensio...  98.1 us
    dot_general x16, matrix products, key_grad_step(): jnp.einsum('qhk,qhd->khd', d_scores, query_block, preferred_element_type=...  89.6 us
  transfers between devices with their start and end apart: 19, of which 14 were waited for; matrix products, arithmetic and copies ran while one was open for 28% of the time, Pallas kernels for 0%

commit v1 on v0

v1 whole, which is shorter than its diff:
```python
import functools
import math

import jax
import jax.numpy as jnp
from jax import lax
from jax.experimental import pallas as pl
from jax.experimental.pallas import tpu as pltpu
from jax.sharding import PartitionSpec as P

HEADS = 12
HEAD_DIM = 64
SPAN = 8
EXT = 16
WIDE = HEAD_DIM + EXT
BIG = 2.0**30
SAFE_SUM = 2.0**100
VMEM = 48 * 2**20

bf16 = jnp.bfloat16
f32 = jnp.float32
norm_eps = 1e-12
base_log = math.log(1000.0)
log2e = math.log2(math.e)


def dot(left_op, right_op, left_dim, right_dim):
    return lax.dot_general(
        left_op, right_op, (((left_dim,), (right_dim,)), ((), ())), preferred_element_type=f32
    )


def ring_order(size):
    return list(range(0, size, 2)) + list(range(size - 1, 0, -2))


def ring_place(index, size):
    return jnp.where(index % 2 == 0, index // 2, size - 1 - index // 2)


def ring_index(place, size):
    place = place % size
    return jnp.where(place < size // 2, 2 * place, 2 * (size - 1 - place) + 1)


def ring_shift(value, step, size):
    order = ring_order(size)
    pairs = [
        (base + order[i], base + order[(i + step) % size])
        for base in range(0, lax.axis_size("fsdp"), size)
        for i in range(size)
    ]
    return lax.ppermute(value, "fsdp", pairs)


def seq_swap(value, mask):
    return lax.ppermute(value, "seq", [(i, i ^ mask) for i in range(lax.axis_size("seq"))])


def arrange_kernel(order, *refs):
    for i, ref in enumerate(refs[:-1]):
        refs[-1][order[i]] = ref[...]


def arrange(blocks, order):
    shape = blocks[0].shape
    return pl.pallas_call(
        arrange_kernel,
        in_specs=[pl.BlockSpec(memory_space=pltpu.SMEM)]
        + [pl.BlockSpec(memory_space=pltpu.VMEM)] * len(blocks),
        out_specs=pl.BlockSpec(memory_space=pltpu.VMEM),
        out_shape=jax.ShapeDtypeStruct((len(blocks),) + shape, blocks[0].dtype),
        compiler_params=pltpu.CompilerParams(vmem_limit_bytes=VMEM),
        name="arrange",
    )(jnp.stack(order).astype(jnp.int32), *blocks)


def ring_gather(block, size, place):
    half = block.shape[0] // 2
    right, left = block, block
    blocks, order = [block], [ring_index(place, size)]
    for t in range(1, size // 2):
        right, left = ring_shift(right, 1, size), ring_shift(left, -1, size)
        blocks += [right, left]
        order += [ring_index(place - t, size), ring_index(place + t, size)]
    last = jnp.concatenate(
        [ring_shift(right[:half], 1, size), ring_shift(left[half:], -1, size)], axis=0
    )
    return arrange(blocks + [last], order + [ring_index(place + size // 2, size)])


def ring_scatter(stacked, size, place):
    def part(offset):
        return lax.dynamic_index_in_dim(stacked, ring_index(place + offset, size), 0, False)

    far = part(size // 2)
    half = far.shape[0] // 2
    right = ring_shift(far[:half], 1, size)
    left = ring_shift(far[half:], -1, size)
    for t in range(size // 2 - 1, 0, -1):
        up, down = part(t).astype(f32), part(-t).astype(f32)
        if t == size // 2 - 1:
            up = jnp.concatenate([up[:half] + right.astype(f32), up[half:]], axis=0)
            down = jnp.concatenate([down[:half], down[half:] + left.astype(f32)], axis=0)
        else:
            up, down = up + right.astype(f32), down + left.astype(f32)
        right = ring_shift(up.astype(bf16), 1, size)
        left = ring_shift(down.astype(bf16), -1, size)
    return part(0).astype(f32) + right.astype(f32) + left.astype(f32)


def three_parts(value):
    high = value.astype(bf16).astype(f32)
    rest = value - high
    mid = rest.astype(bf16).astype(f32)
    return high, mid, rest - mid


def with_parts(base, value):
    high, mid, low = three_parts(value)
    lane = lax.broadcasted_iota(jnp.int32, base.shape, 1)
    filled = jnp.where(lane == HEAD_DIM, high, base)
    filled = jnp.where(lane == HEAD_DIM + 1, mid, filled)
    return jnp.where(lane == HEAD_DIM + 2, low, filled)


def first_kernel(heads, tile, qt_ref, qe_ref, k_ref, v_ref, ke_ref, qx_ref, acc_ref):
    ones = jnp.ones((EXT, k_ref.shape[1]), bf16)
    for h in range(heads):
        rows = slice(h * HEAD_DIM, (h + 1) * HEAD_DIM)
        keys = jnp.concatenate([k_ref[rows, :], ke_ref[...]], axis=0)
        vals = jnp.concatenate([v_ref[rows, :], ones], axis=0)
        for start in range(0, qt_ref.shape[1], tile):
            cut = slice(start, start + tile)
            natural = qt_ref[rows, cut].astype(f32).T
            queries = jnp.concatenate([natural, qe_ref[cut, :].astype(f32)], axis=1)
            scores = dot(queries.astype(bf16), keys, 1, 0)
            top = jnp.max(scores, axis=1, keepdims=True)
            weights = jnp.exp2(scores - top).astype(bf16)
            acc_ref[h, :, cut] = dot(vals, weights, 1, 1)
            qx_ref[h, cut, :] = with_parts(queries, top).astype(bf16)


def step_kernel(heads, tile, count, *refs):
    qx_ref, acc_in, acc_ref = refs[0], refs[1], refs[-1]
    blocks = refs[2:-1]
    ones = jnp.ones((EXT, blocks[0].shape[1]), bf16)
    for h in range(heads):
        rows = slice(h * HEAD_DIM, (h + 1) * HEAD_DIM)
        pairs = []
        for b in range(count):
            k_ref, v_ref, ke_ref = blocks[3 * b : 3 * b + 3]
            pairs.append(
                (
                    jnp.concatenate([k_ref[rows, :], ke_ref[...]], axis=0),
                    jnp.concatenate([v_ref[rows, :], ones], axis=0),
                )
            )
        for start in range(0, qx_ref.shape[1], tile):
            cut = slice(start, start + tile)
            total = acc_in[h, :, cut]
            for keys, vals in pairs:
                weights = jnp.exp2(dot(qx_ref[h, cut, :], keys, 1, 0)).astype(bf16)
                total = total + dot(vals, weights, 1, 1)
            acc_ref[h, :, cut] = total


def finish_kernel(heads, tile, count, *refs):
    qx_ref, acc_ref, ke_ref = refs[:3]
    blocks = refs[3 : 3 + 2 * count]
    ot_ref, on_ref, qx2_ref, k_buf, v_buf, acc, qx = refs[3 + 2 * count :]
    length = qx_ref.shape[1]
    sums = jnp.concatenate([acc_ref[h, HEAD_DIM : HEAD_DIM + 8, :] for h in range(heads)], axis=0)
    fine = jnp.logical_and(sums <= SAFE_SUM, sums >= 0.5)
    good = jnp.min(jnp.where(fine, 1.0, 0.0)) > 0.5
    acc[...] = acc_ref[...]
    qx[...] = qx_ref[...]

    @pl.when(jnp.logical_not(good))
    def _():
        ones = jnp.ones((EXT, k_buf.shape[1]), bf16)
        lane = lax.broadcasted_iota(jnp.int32, (tile, WIDE), 1)
        inside = jnp.logical_and(lane >= HEAD_DIM, lane < HEAD_DIM + 3)

        def each(body):
            for b in range(count):
                pltpu.sync_copy(blocks[2 * b], k_buf)
                pltpu.sync_copy(blocks[2 * b + 1], v_buf)

                def turn(step, carry):
                    h = step // (length // tile)
                    cut = pl.ds(pl.multiple_of(step % (length // tile) * tile, tile), tile)
                    rows = pl.ds(pl.multiple_of(h * HEAD_DIM, HEAD_DIM), HEAD_DIM)
                    keys = jnp.concatenate([k_buf[rows, :], ke_ref[b]], axis=0)
                    vals = jnp.concatenate([v_buf[rows, :], ones], axis=0)
                    body(b, h, cut, keys, vals)
                    return carry

                lax.fori_loop(0, heads * (length // tile), turn, 0)

        def raise_top(b, h, cut, keys, vals):
            base = qx[h, cut, :].astype(f32)
            old = jnp.sum(jnp.where(inside, base, 0.0), axis=1, keepdims=True)
            plain = jnp.where(inside, 0.0, base)
            scores = dot(plain.astype(bf16), keys, 1, 0)
            top = jnp.maximum(old, jnp.max(scores, axis=1, keepdims=True))
            qx[h, cut, :] = with_parts(plain, top).astype(bf16)

        def add_up(b, h, cut, keys, vals):
            weights = jnp.exp2(dot(qx[h, cut, :], keys, 1, 0)).astype(bf16)
            acc[h, :, cut] += dot(vals, weights, 1, 1)

        each(raise_top)
        acc[...] = jnp.zeros_like(acc)
        each(add_up)

    for h in range(heads):
        rows = slice(h * HEAD_DIM, (h + 1) * HEAD_DIM)
        for start in range(0, length, tile):
            cut = slice(start, start + tile)
            block = acc[h, :, cut]
            total = block[HEAD_DIM : HEAD_DIM + 1, :]
            ot_ref[rows, cut] = (block[:HEAD_DIM, :] / total).astype(bf16)
            natural = block.T
            sums = natural[:, HEAD_DIM : HEAD_DIM + 1]
            on_ref[h, cut, :] = natural[:, :HEAD_DIM] / sums
            base = qx[h, cut, :].astype(f32)
            lane = lax.broadcasted_iota(jnp.int32, base.shape, 1)
            inside = jnp.logical_and(lane >= HEAD_DIM, lane < HEAD_DIM + 3)
            top = jnp.sum(jnp.where(inside, base, 0.0), axis=1, keepdims=True)
            qx2_ref[h, cut, :] = with_parts(base, top + jnp.log2(sums)).astype(bf16)


def delta_kernel(heads, tile, dot_ref, on_ref, dox_ref):
    for h in range(heads):
        rows = slice(h * HEAD_DIM, (h + 1) * HEAD_DIM)
        for start in range(0, dot_ref.shape[1], tile):
            cut = slice(start, start + tile)
            natural = dot_ref[rows, cut].astype(f32).T
            delta = jnp.sum(natural * on_ref[h, cut, :], axis=1, keepdims=True)
            base = jnp.concatenate([natural, jnp.zeros((tile, EXT), f32)], axis=1)
            dox_ref[h, cut, :] = with_parts(base, delta).astype(bf16)


def back_kernel(
    heads,
    q_tile,
    k_tile,
    qx_ref,
    dox_ref,
    qt_ref,
    dot_ref,
    dq_in,
    k_ref,
    v_ref,
    ke_ref,
    dq_ref,
    dk_ref,
    dv_ref,
):
    for h in range(heads):
        rows = slice(h * HEAD_DIM, (h + 1) * HEAD_DIM)
        keys = jnp.concatenate([k_ref[rows, :], ke_ref[...]], axis=0)
        vals = jnp.concatenate([v_ref[rows, :], ke_ref[...]], axis=0)
        for k_start in range(0, k_ref.shape[1], k_tile):
            k_cut = slice(k_start, k_start + k_tile)
            d_key, d_value = 0.0, 0.0
            for start in range(0, qt_ref.shape[1], q_tile):
                cut = slice(start, start + q_tile)
                weights = jnp.exp2(dot(qx_ref[h, cut, :], keys[:, k_cut], 1, 0))
                shifted = dot(dox_ref[h, cut, :], vals[:, k_cut], 1, 0)
                d_scores = (weights * shifted).astype(bf16)
                d_value = d_value + dot(dot_ref[rows, cut], weights.astype(bf16), 1, 0)
                d_key = d_key + dot(qt_ref[rows, cut], d_scores, 1, 0)
                d_query = dot(keys[:HEAD_DIM, k_cut], d_scores, 1, 1)
                if k_start == 0:
                    dq_ref[rows, cut] = dq_in[rows, cut] + d_query
                else:
                    dq_ref[rows, cut] += d_query
            dk_ref[rows, k_cut] = d_key.astype(bf16)
            dv_ref[rows, k_cut] = d_value.astype(bf16)


def local_call(kernel, outs, ins, flops, name, scratch=(), spaces=None):
    spaces = spaces or [pltpu.VMEM] * len(ins)
    return pl.pallas_call(
        kernel,
        in_specs=[pl.BlockSpec(memory_space=space) for space in spaces],
        out_specs=[pl.BlockSpec(memory_space=pltpu.VMEM) for _ in outs],
        out_shape=[jax.ShapeDtypeStruct(shape, dtype) for shape, dtype in outs],
        scratch_shapes=list(scratch),
        compiler_params=pltpu.CompilerParams(vmem_limit_bytes=VMEM),
        cost_estimate=pl.CostEstimate(flops=flops, bytes_accessed=2**20, transcendentals=0),
        name=name,
    )(*ins)


def layer_norm(rows_in):
    centre = rows_in - jnp.mean(rows_in, axis=-1, keepdims=True)
    spread = jnp.mean(centre * centre, axis=-1, keepdims=True)
    rstd = lax.rsqrt(spread + norm_eps)
    return centre * rstd, rstd


def norm_back(normed, rstd, grad, gain):
    scaled = grad * gain
    return rstd * (
        scaled
        - jnp.mean(scaled, axis=-1, keepdims=True)
        - normed * jnp.mean(scaled * normed, axis=-1, keepdims=True)
    )


def turn(part, cosine, sine):
    heads = part.shape[0] // HEAD_DIM
    split = part.reshape(heads, 2, HEAD_DIM // 2, part.shape[1])
    lead, tail = split[:, 0], split[:, 1]
    return jnp.stack([lead * cosine - tail * sine, tail * cosine + lead * sine], 1).reshape(
        part.shape
    )


def local(
    layer_input,
    out_grad,
    doc_ids,
    w_qkv,
    w_out,
    norm1_gain,
    norm1_bias,
    w_up,
    w_gate,
    w_down,
    norm2_gain,
    norm2_bias,
):
    fsdp = lax.axis_size("fsdp")
    groups = lax.axis_size("seq")
    f = lax.axis_index("fsdp")
    s = lax.axis_index("seq")
    side, core = s // 2, s % 2
    tok_rows, width = layer_input.shape
    w_rows = w_qkv.shape[0]
    inner = width // groups
    heads = inner // HEAD_DIM
    group_rows = tok_rows * groups
    half_rows = group_rows // 2
    length = SPAN * group_rows
    place = ring_place(f, fsdp)
    spot = ring_place(f % SPAN, SPAN)
    base = f // SPAN * SPAN

    def quarter(matrix, start):
        return lax.dynamic_slice_in_dim(matrix, start + s * inner, inner, 1)

    qkv_own = jnp.concatenate([quarter(w_qkv, i * width) for i in range(3)], axis=1).astype(bf16)
    x_side = seq_swap(layer_input, 2)
    x_core = seq_swap(layer_input, 1)
    x_far = seq_swap(x_side, 1)
    qkv_full = ring_gather(qkv_own, fsdp, place).reshape(width, 3 * inner)

    def ff_quarter(matrix):
        split = matrix.reshape(w_rows, fsdp, groups, w_rows)
        return lax.dynamic_index_in_dim(split, s, 2, False).reshape(w_rows, width)

    gains = jnp.stack([norm1_gain, norm1_bias, norm2_gain, norm2_bias], axis=1)
    own = jnp.concatenate(
        [
            w_out,
            ff_quarter(w_up),
            ff_quarter(w_gate),
            lax.dynamic_slice_in_dim(w_down, s * w_rows, w_rows, 0),
            gains,
            jnp.zeros((w_rows, 124), f32),
        ],
        axis=1,
    ).astype(bf16)
    full = ring_gather(own, fsdp, place).reshape(width, own.shape[1])
    out_full = full[:, :width]
    up_own = full[:, width : 2 * width]
    gate_own = full[:, 2 * width : 3 * width]
    down_own = full[:, 3 * width : 4 * width]
    vectors = full[:, 4 * width : 4 * width + 4].astype(f32).T
    gain_one, bias_one, gain_two, bias_two = [vectors[i : i + 1] for i in range(4)]
    up_other = seq_swap(up_own, 2)
    gate_other = seq_swap(gate_own, 2)
    down_other = seq_swap(down_own, 2)

    x_all = arrange([layer_input, x_side, x_core, x_far], [s, s ^ 2, s ^ 1, s ^ 3]).reshape(
        group_rows, width
    )
    projected = dot(qkv_full, x_all, 0, 1)
    positions = f % SPAN * group_rows + jnp.arange(group_rows, dtype=jnp.int32)
    steps = jnp.arange(HEAD_DIM // 2, dtype=f32)
    freqs = jnp.exp(steps * (-2.0 * base_log / HEAD_DIM))
    angles = freqs[:, None] * positions.astype(f32)[None, :]
    cosine, sine = jnp.cos(angles), jnp.sin(angles)
    score_scale = HEAD_DIM ** (-0.5)
    queries = turn(projected[:inner] * (score_scale * log2e), cosine, sine).astype(bf16)
    own_kv = jnp.concatenate(
        [turn(projected[inner : 2 * inner], cosine, sine), projected[2 * inner :]], axis=0
    ).astype(bf16)

    seq_docs = lax.dynamic_slice_in_dim(doc_ids, f // SPAN * length, length) - f // SPAN * 3
    kinds = jnp.arange(3, dtype=jnp.int32)
    key_ext = jnp.concatenate(
        [
            jnp.full((3, length), -1.0, f32),
            jnp.where(seq_docs[None, :] == kinds[:, None], 0.0, -1.0),
            jnp.zeros((EXT - 6, length), f32),
        ],
        axis=0,
    ).astype(bf16)
    own_docs = lax.dynamic_slice_in_dim(seq_docs, f % SPAN * group_rows, group_rows)
    query_ext = jnp.concatenate(
        [
            jnp.zeros((group_rows, 3), f32),
            jnp.where(own_docs[:, None] == kinds[None, :], BIG, 0.0),
            jnp.zeros((group_rows, EXT - 6), f32),
        ],
        axis=1,
    ).astype(bf16)

    def ext_of(offset):
        return lax.dynamic_slice_in_dim(
            key_ext, ring_index(spot + offset, SPAN) * group_rows, group_rows, 1
        )

    block_flops = 4 * 256 * heads * group_rows * group_rows // 2
    acc_out = ((heads, WIDE, group_rows), f32)
    wide_out = ((heads, group_rows, WIDE), bf16)
    tile = min(512, group_rows)
    own_ext = ext_of(0)
    qx, acc = local_call(
        functools.partial(first_kernel, heads, tile),
        [wide_out, acc_out],
        [queries, query_ext, own_kv[:inner], own_kv[inner:], own_ext],
        block_flops,
        "attend_own",
    )
    blocks = {0: (own_kv[:inner], own_kv[inner:], own_ext)}
    right, left = own_kv, own_kv
    for t in range(1, SPAN // 2 + 1):
        if t < SPAN // 2:
            right, left = ring_shift(right, 1, SPAN), ring_shift(left, -1, SPAN)
            blocks[-t] = (right[:inner], right[inner:], ext_of(-t))
            blocks[t] = (left[:inner], left[inner:], ext_of(t))
            now = blocks[-t] + blocks[t]
        else:
            blocks[t] = (
                ring_shift(right[:inner], 1, SPAN),
                ring_shift(left[inner:], -1, SPAN),
                ext_of(t),
            )
            now = blocks[t]
        (acc,) = local_call(
            functools.partial(step_kernel, heads, tile, len(now) // 3),
            [acc_out],
            [qx, acc, *now],
            block_flops * (len(now) // 3),
            "attend_step",
        )
    offsets = sorted(blocks)
    heads_t, heads_n, qx = local_call(
        functools.partial(finish_kernel, heads, min(256, group_rows), SPAN),
        [((inner, group_rows), bf16), ((heads, group_rows, HEAD_DIM), f32), wide_out],
        [
            qx,
            acc,
            jnp.stack([blocks[o][2] for o in offsets]),
            *[ref for o in offsets for ref in blocks[o][:2]],
        ],
        block_flops // 16,
        "attend_finish",
        scratch=[
            pltpu.VMEM((inner, group_rows), bf16),
            pltpu.VMEM((inner, group_rows), bf16),
            pltpu.VMEM(*acc_out),
            pltpu.VMEM(*wide_out),
        ],
        spaces=[pltpu.VMEM] * 3 + [pl.ANY] * (2 * SPAN),
    )

    def my_half(value, axis):
        return lax.dynamic_slice_in_dim(value, side * half_rows, half_rows, axis)

    def other_half(value, axis):
        return lax.dynamic_slice_in_dim(value, (1 - side) * half_rows, half_rows, axis)

    heads_own = my_half(heads_t, 1)
    heads_side = seq_swap(other_half(heads_t, 1), 2)
    heads_pair = jnp.stack([heads_own, heads_side])
    heads_far = seq_swap(heads_pair, 1)
    heads_all = arrange(
        [heads_own, heads_side, heads_far[0], heads_far[1]], [s, s ^ 2, s ^ 1, s ^ 3]
    ).reshape(width, half_rows)
    x_half = my_half(x_all, 0).astype(f32)
    first_sum = x_half + dot(heads_all, out_full, 0, 0)
    normed_one, rstd_one = layer_norm(first_sum)
    hidden = normed_one * gain_one + bias_one
    hidden_low = hidden.astype(bf16)

    def my_rows(value):
        return lax.dynamic_slice_in_dim(value, core * tok_rows, tok_rows, 0)

    def other_rows(value):
        return lax.dynamic_slice_in_dim(value, (1 - core) * tok_rows, tok_rows, 0)

    def core_sum(value):
        got = seq_swap(other_rows(value).astype(bf16), 1)
        return my_rows(value) + got.astype(f32)

    def core_gather(value):
        got = seq_swap(value, 1)
        return arrange([value, got], [core, 1 - core]).reshape(half_rows, width)

    acts = []
    branch = 0.0
    for up_w, gate_w, down_w in ((up_own, gate_own, down_own), (up_other, gate_other, down_other)):
        up_act, gate_act = dot(hidden_low, up_w, 1, 0), dot(hidden_low, gate_w, 1, 0)
        gate_sig = lax.logistic(gate_act)
        inner_low = (gate_act * gate_sig * up_act).astype(bf16)
        acts.append((up_act, gate_act, gate_sig, inner_low))
        branch = branch + dot(inner_low, down_w, 1, 0)
    second_sum = my_rows(hidden) + core_sum(branch)
    normed_two, rstd_two = layer_norm(second_sum)
    result = normed_two * gain_two + bias_two
    cotangent = out_grad.astype(f32)
    d_second = norm_back(normed_two, rstd_two, cotangent, gain_two)
    d_branch_two = core_gather(d_second.astype(bf16))
    d_hidden = 0.0
    ff_grads = []
    for (up_act, gate_act, gate_sig, inner_low), (up_w, gate_w, down_w) in zip(
        acts, ((up_own, gate_own, down_own), (up_other, gate_other, down_other))
    ):
        d_inner = dot(d_branch_two, down_w, 1, 1)
        d_gate = (d_inner * up_act * gate_sig * (1.0 + gate_act * (1.0 - gate_sig))).astype(bf16)
        d_up = (d_inner * gate_act * gate_sig).astype(bf16)
        d_hidden = d_hidden + dot(d_up, up_w, 1, 1) + dot(d_gate, gate_w, 1, 1)
        ff_grads.append(
            (
                dot(hidden_low, d_up, 0, 0),
                dot(hidden_low, d_gate, 0, 0),
                dot(inner_low, d_branch_two, 0, 0),
            )
        )
    d_hidden = d_second + core_sum(d_hidden)
    normed_own = my_rows(normed_one)
    d_first = norm_back(normed_own, my_rows(rstd_one), d_hidden, gain_one)
    d_branch_one = core_gather(d_first.astype(bf16))

    def out_rows(which):
        return lax.dynamic_slice_in_dim(out_full, (2 * which + core) * inner, inner, 0)

    d_heads_own = dot(out_rows(side), d_branch_one, 1, 1).astype(bf16)
    d_heads_side = seq_swap(dot(out_rows(1 - side), d_branch_one, 1, 1).astype(bf16), 2)
    d_heads_t = jnp.concatenate(
        [
            jnp.where(side == 0, d_heads_own, d_heads_side),
            jnp.where(side == 0, d_heads_side, d_heads_own),
        ],
        axis=1,
    )
    (dox,) = local_call(
        functools.partial(delta_kernel, heads, tile),
        [wide_out],
        [d_heads_t, heads_n],
        block_flops // 16,
        "delta",
    )

    def out_columns(which):
        return lax.dynamic_slice_in_dim(d_branch_one, (2 * which + core) * inner, inner, 1)

    grad_vectors = jnp.stack(
        [
            jnp.sum(d_hidden * normed_own, axis=0),
            jnp.sum(d_hidden, axis=0),
            jnp.sum(cotangent * normed_two, axis=0),
            jnp.sum(cotangent, axis=0),
        ],
        axis=1,
    )
    own_grads = [*ff_grads[0], dot(heads_all, out_columns(side), 1, 0)]
    other_grads = [*ff_grads[1], dot(heads_all, out_columns(1 - side), 1, 0)]
    got_grads = [seq_swap(grad.astype(bf16), 2) for grad in other_grads]
    summed = [
        (mine + got.astype(f32)).astype(bf16).reshape(fsdp, w_rows, -1)
        for mine, got in zip(own_grads, got_grads)
    ]
    packed = jnp.concatenate(
        summed
        + [
            grad_vectors.astype(bf16).reshape(fsdp, w_rows, 4),
            jnp.zeros((fsdp, w_rows, 60), bf16),
        ],
        axis=2,
    )
    grads_own = ring_scatter(packed, fsdp, place).astype(bf16)

    d_query = jnp.zeros((inner, group_rows), f32)

    def back(offset, d_query):
        return local_call(
            functools.partial(back_kernel, heads, min(256, group_rows), group_rows),
            [((inner, group_rows), f32), ((inner, group_rows), bf16), ((inner, group_rows), bf16)],
            [qx, dox, queries, d_heads_t, d_query, *blocks[offset]],
            block_flops * 2,
            "attend_back",
        )

    far = SPAN // 2
    d_query, d_key, d_value = back(far, d_query)
    right, left = ring_shift(d_key, 1, SPAN), ring_shift(d_value, -1, SPAN)
    for t in range(far - 1, 0, -1):
        d_query, up_key, up_value = back(t, d_query)
        d_query, down_key, down_value = back(-t, d_query)
        if t == far - 1:
            up = jnp.concatenate([(up_key + right), up_value], axis=0)
            down = jnp.concatenate([down_key, (down_value + left)], axis=0)
        else:
            up = jnp.concatenate([up_key, up_value], axis=0) + right
            down = jnp.concatenate([down_key, down_value], axis=0) + left
        right, left = ring_shift(up, 1, SPAN), ring_shift(down, -1, SPAN)
    d_query, d_key, d_value = back(0, d_query)
    d_kv = (
        jnp.concatenate([d_key, d_value], axis=0).astype(f32) + right.astype(f32) + left.astype(f32)
    )
    d_raw_q = turn(d_query * score_scale, cosine, -sine)
    d_raw_k = turn(d_kv[:inner] * (1.0 / log2e), cosine, -sine)
    d_projected = jnp.concatenate([d_raw_q, d_raw_k, d_kv[inner:]], axis=0).astype(bf16)

    grad_qkv = dot(x_all, d_projected, 0, 1).astype(bf16).reshape(fsdp, w_rows, 3 * inner)
    qkv_own_grad = ring_scatter(grad_qkv, fsdp, place).astype(bf16)
    d_input = dot(d_projected, qkv_full, 0, 1).reshape(2, 2, tok_rows, width)
    sent = lax.dynamic_index_in_dim(d_input, 1 - core, 1, False).astype(bf16)
    kept = lax.dynamic_index_in_dim(d_input, core, 1, False)
    d_input = kept + seq_swap(sent, 1).astype(f32)
    sent = lax.dynamic_index_in_dim(d_input, 1 - side, 0, False).astype(bf16)
    kept = lax.dynamic_index_in_dim(d_input, side, 0, False)
    d_input = d_first + kept + seq_swap(sent, 2).astype(f32)

    def seq_gather(value):
        pair = jnp.stack([value, seq_swap(value, 2)])
        far_pair = seq_swap(pair, 1)
        return arrange([pair[0], pair[1], far_pair[0], far_pair[1]], [s, s ^ 2, s ^ 1, s ^ 3])

    qkv_parts = seq_gather(qkv_own_grad).astype(f32)
    parts = seq_gather(grads_own).astype(f32)
    final_qkv = qkv_parts.reshape(groups, w_rows, 3, inner).transpose(1, 2, 0, 3)
    final_up = parts[:, :, :width].reshape(groups, w_rows, fsdp, w_rows).transpose(1, 2, 0, 3)
    final_gate = (
        parts[:, :, width : 2 * width].reshape(groups, w_rows, fsdp, w_rows).transpose(1, 2, 0, 3)
    )
    final_down = parts[:, :, 2 * width : 3 * width].reshape(groups * w_rows, width)
    final_out = parts[:, :, 3 * width : 3 * width + inner].transpose(1, 0, 2)
    final_vectors = jnp.sum(
        parts[:, :, 3 * width + inner : 3 * width + inner + 4], axis=0
    ).T
    return (
        result.astype(bf16),
        d_input.astype(bf16),
        final_qkv.reshape(w_rows, 3 * width),
        final_out.reshape(w_rows, width),
        final_vectors[0],
        final_vectors[1],
        final_up.reshape(w_rows, -1),
        final_gate.reshape(w_rows, -1),
        final_down,
        final_vectors[2],
        final_vectors[3],
    )


def solution(mesh):
    rows = P(("fsdp", "seq"), None)
    param, vector = P("fsdp", None), P("fsdp")
    in_specs = (rows, rows, P(), param, param, vector, vector, param, param, param, vector, vector)
    out_specs = (rows, rows, param, param, vector, vector, param, param, param, vector, vector)
    return jax.shard_map(local, mesh=mesh, in_specs=in_specs, out_specs=out_specs, check_vma=False)
```

time: 1820 us -> 653 us (0.36)
  waiting for transfers between devices: 783 us -> 289 us
  matrix products: 502 us -> 50 us
  blocking collectives: 298 us -> 0 us
  Pallas kernels: 0 us -> 106 us
  starting transfers between devices: 14.7 us -> 70.9 us
  other arithmetic: 81.8 us -> 32.8 us
  local copies, waits for them, and re-layouts: 112 us -> 91.8 us
    dot_general x127 -> x26, matrix products: 502 us -> 50 us  [dot(): lax.dot_general(left_op, right_op, (((left_dim,), (right_dim,)), ((), ())...]
    reduce_scatter x4 -> x0, waiting for transfers between devices: 361 us -> none  [the longest x1 98.7 us: local(): lax.psum_scatter(grad_up.astype(jnp.bfloat16), 'fsdp', scatter_dimension=...]
    all_gather x2 -> x0, blocking collectives: 180 us -> none  [the longest x1 149 us: local(): lax.all_gather(log_total, 'fsdp', axis=0, tiled=True)]
    pallas_call x0 -> x23, Pallas kernels: none -> 106 us  [the longest x15 97.4 us: local_call(): pl.pallas_call(kernel, in_specs=[pl.BlockSpec(memory_space=space) for spa...]
    all_gather x5 -> x0, waiting for transfers between devices: 80.4 us -> none  [the longest x1 64.1 us: local(): lax.all_gather(w_qkv.astype(jnp.bfloat16), 'fsdp', axis=0, tiled=True)]
    ppermute x6 -> x71, starting transfers between devices: 5.82 us -> 70.9 us  [the longest x48 52.5 us: ring_shift(): return lax.ppermute(value, 'fsdp', pairs)]
    unnamed x2 -> x0, blocking collectives: 64.2 us -> none
    unnamed x12 -> x0, waiting for transfers between devices: 63 us -> none
  transfers between devices with their start and end apart: 19 -> 71, of which waited for: 14 -> 35; matrix products, arithmetic and copies ran while one was open for 28% -> 18% of each run, Pallas kernels for 0% -> 14%
where the time goes in v1:
time: 653 us; the launch traced here: 644 us
  waiting for transfers between devices  289 us (44%)
  Pallas kernels  106 us (16%)
  local copies, waits for them, and re-layouts  91.8 us (14%)
  starting transfers between devices  70.9 us (11%)
  matrix products  50 us (8%)
  other arithmetic  32.8 us (5%)
    ppermute x48, waiting for transfers between devices, ring_shift(): return lax.ppermute(value, 'fsdp', pairs)  145 us
    ppermute x23, waiting for transfers between devices, seq_swap(): lax.ppermute(value, 'seq', [(i, i ^ mask) for i in range(lax.axis_size('s...  144 us
    pallas_call x15, Pallas kernels, local_call(): pl.pallas_call(kernel, in_specs=[pl.BlockSpec(memory_space=space) for spa...  97.4 us
    ppermute x48, starting transfers between devices, ring_shift(): return lax.ppermute(value, 'fsdp', pairs)  52.5 us
    dot_general x26, matrix products, dot(): lax.dot_general(left_op, right_op, (((left_dim,), (right_dim,)), ((), ())...  50 us
    unnamed x326, local copies, waits for them, and re-layouts  24.2 us
    ppermute x23, starting transfers between devices, seq_swap(): lax.ppermute(value, 'seq', [(i, i ^ mask) for i in range(lax.axis_size('s...  18.5 us
  transfers between devices with their start and end apart: 71, of which 35 were waited for; matrix products, arithmetic and copies ran while one was open for 18% of the time, Pallas kernels for 14%

profile of v1, /device:TPU:0, one launch (start us, length us, event | category | flops | bytes accessed | tf_op | source)
XLA Modules:
  0.0 644.3 jit_solution(2634553419281113243)
XLA Ops:
  7.6 3.3 reshape.343
  24.2 11.5 %collective-permute-done.6.refs_4_ = bf16[96,576]{1,0:T(8,128)(2,1)S(1)} collective-permute-done((bf16[96,576]{1,0:T(8,128)(2,1)S(1)}, bf16[96,576]{1,0:T(8,128)(2,1)S(1)}, u32[]{:S(2)}, u32[]{:S(2)}) %collective-permute-start.6) | collective-permute-done | bytes 110624 | tf_op jit(solution)/shard_map/ppermute | solution.py:53
  36.7 3.9 collective-permute-done.8.refs_6_
  65.0 7.6 %collective-permute-done.23.refs_3_ = bf16[96,3200]{1,0:T(8,128)(2,1)S(1)} collective-permute-done((bf16[96,3200]{1,0:T(8,128)(2,1)}, bf16[96,3200]{1,0:T(8,128)(2,1)S(1)}, u32[]{:S(2)}, u32[]{:S(2)}) %collective-permute-start.23) | collective-permute-done | bytes 614432 | tf_op jit(solution)/shard_map/ppermute | solution.py:53
  75.1 5.1 attend_own.1
  80.2 10.8 %collective-permute-done.12 = bf16[384,1024]{1,0:T(8,128)(2,1)S(1)} collective-permute-done((bf16[384,1024]{1,0:T(8,128)(2,1)S(1)}, bf16[384,1024]{1,0:T(8,128)(2,1)S(1)}, u32[]{:S(2)}, u32[]{:S(2)}) %collective-permute-start.12) | collective-permute-done | bytes 786464 | tf_op jit(solution)/shard_map/ppermute | solution.py:53
  93.1 9.5 %collective-permute-done.25.refs_5_ = bf16[96,3200]{1,0:T(8,128)(2,1)S(1)} collective-permute-done((bf16[96,3200]{1,0:T(8,128)(2,1)S(1)}, bf16[96,3200]{1,0:T(8,128)(2,1)S(1)}, u32[]{:S(2)}, u32[]{:S(2)}) %collective-permute-start.25) | collective-permute-done | bytes 614432 | tf_op jit(solution)/shard_map/ppermute | solution.py:53
  104.9 6.5 %attend_step.4.refs_1_ = f32[3,80,1024]{2,1,0:T(8,128)S(1)} custom-call(bf16[3,1024,80]{2,1,0:T(8,128)(2,1)S(1)} %get-tuple-element.40.refs_0_, f32[3,80,1024]{2,1,0:T(8,128)S(1)} %get-tuple-element.41.refs_1_, bf16[192,1024]{1,0:T(8,128)(2,1)S(1)} %get-tuple-element.160.refs_2_.refs_7_.k_ref, ...), custom_call_target="tpu_custom_call" | custom-call | flops 3221225472 | bytes 1048576 | tf_op jit(solution)/shard_map/attend_step/pallas_call | solution.py:286
  111.4 9.7 %collective-permute-done.14 = bf16[384,1024]{1,0:T(8,128)(2,1)} collective-permute-done((bf16[384,1024]{1,0:T(8,128)(2,1)S(1)}, bf16[384,1024]{1,0:T(8,128)(2,1)}, u32[]{:S(2)}, u32[]{:S(2)}) %collective-permute-start.14) | collective-permute-done | bytes 786464 | tf_op jit(solution)/shard_map/ppermute | solution.py:53
  127.7 3.8 arrange.11
  132.7 6.1 collective-permute-done.15
  143.6 6.5 %attend_step.5.refs_1_ = f32[3,80,1024]{2,1,0:T(8,128)S(1)} custom-call(bf16[3,1024,80]{2,1,0:T(8,128)(2,1)S(1)} %get-tuple-element.40.refs_0_, f32[3,80,1024]{2,1,0:T(8,128)S(1)} %copy-done.87, bf16[192,1024]{1,0:T(8,128)(2,1)S(1)} %get-tuple-element.156.refs_2_.refs_5_.k_ref, bf16[192,1024]{1,0:T(8,128)(2,1)S(1)} %get-tuple-element.155.refs_3_.refs_6_.v_ref, ...), custom_call_target="tpu_custom_call" | custom-call | flops 3221225472 | bytes 1048576 | tf_op jit(solution)/shard_map/attend_step/pallas_call | solution.py:286
  150.1 6.5 %attend_step.6.refs_1_ = f32[3,80,1024]{2,1,0:T(8,128)S(1)} custom-call(bf16[3,1024,80]{2,1,0:T(8,128)(2,1)S(1)} %get-tuple-element.40.refs_0_, f32[3,80,1024]{2,1,0:T(8,128)S(1)} %attend_step.5.refs_1_, bf16[192,1024]{1,0:T(8,128)(2,1)S(1)} %get-tuple-element.152.refs_2_.refs_3_.k_ref, bf16[192,1024]{1,0:T(8,128)(2,1)S(1)} %get-tuple-element.151.refs_3_.refs_4_.v_ref, ...), custom_call_target="tpu_custom_call" | custom-call | flops 3221225472 | bytes 1048576 | tf_op jit(solution)/shard_map/attend_step/pallas_call | solution.py:286
  156.7 3.5 attend_step.7.refs_1_
  161.3 9.8 %attend_finish.1 = (bf16[192,1024]{1,0:T(8,128)(2,1)S(1)}, f32[3,1024,64]{2,1,0:T(8,128)}, bf16[3,1024,80]{2,1,0:T(8,128)(2,1)}) custom-call(bf16[3,1024,80]{2,1,0:T(8,128)(2,1)} %copy-done.33, f32[3,80,1024]{2,1,0:T(8,128)} %copy-done.29, bf16[8,16,1024]{2,1,0:T(8,128)(2,1)S(1)} %get-tuple-element.90.refs_2_, ...), custom_call_target="tpu_custom_call" | custom-call | flops 100663296 | bytes 1048576 | tf_op jit(solution)/shard_map/attend_finish/pallas_call | solution.py:286
  173.8 3.0 collective-permute-done.19.refs_1_
  176.9 3.8 fusion.58
  189.8 19.7 %collective-permute-done.29 = bf16[768,768]{1,0:T(8,128)(2,1)S(1)} collective-permute-done((bf16[768,768]{1,0:T(8,128)(2,1)S(1)}, bf16[768,768]{1,0:T(8,128)(2,1)S(1)}, u32[]{:S(2)}, u32[]{:S(2)}) %collective-permute-start.29) | collective-permute-done | bytes 1179680 | tf_op jit(solution)/shard_map/ppermute | solution.py:57
  210.6 24.4 %collective-permute-done.30 = bf16[768,768]{1,0:T(8,128)(2,1)} collective-permute-done((bf16[768,768]{1,0:T(8,128)(2,1)S(1)}, bf16[768,768]{1,0:T(8,128)(2,1)}, u32[]{:S(2)}, u32[]{:S(2)}) %collective-permute-start.30) | collective-permute-done | bytes 1179680 | tf_op jit(solution)/shard_map/ppermute | solution.py:57
  234.9 3.3 multiply_convert_fusion.4
  240.2 19.4 %collective-permute-done.31 = bf16[768,768]{1,0:T(8,128)(2,1)} collective-permute-done((bf16[768,768]{1,0:T(8,128)(2,1)S(1)}, bf16[768,768]{1,0:T(8,128)(2,1)}, u32[]{:S(2)}, u32[]{:S(2)}) %collective-permute-start.31) | collective-permute-done | bytes 1179680 | tf_op jit(solution)/shard_map/ppermute | solution.py:57
  292.8 3.4 convolution_convert_fusion
  296.3 3.3 multiply_reduce_fusion.1
  316.4 70.4 %collective-permute-done.36 = bf16[192,512]{1,0:T(8,128)(2,1)S(1)} collective-permute-done((bf16[192,512]{1,0:T(8,128)(2,1)S(1)}, bf16[192,512]{1,0:T(8,128)(2,1)S(1)}, u32[]{:S(2)}, u32[]{:S(2)}) %collective-permute-start.36) | collective-permute-done | bytes 196640 | tf_op jit(solution)/shard_map/ppermute | solution.py:57
  388.8 7.4 %attend_back.8 = (f32[192,1024]{1,0:T(8,128)S(1)}, bf16[192,1024]{1,0:T(8,128)(2,1)S(1)}, bf16[192,1024]{1,0:T(8,128)(2,1)S(1)}) custom-call(bf16[3,1024,80]{2,1,0:T(8,128)(2,1)S(1)} %copy-done.79, bf16[3,1024,80]{2,1,0:T(8,128)(2,1)S(1)} %delta.1.dox_ref, bf16[192,1024]{1,0:T(8,128)(2,1)S(1)} %bitcast.251, ...), custom_call_target="tpu_custom_call" | custom-call | flops 3221225472 | bytes 1048576 | tf_op jit(solution)/shard_map/attend_back/pallas_call | solution.py:286
  397.7 7.2 %attend_back.9 = (f32[192,1024]{1,0:T(8,128)S(1)}, bf16[192,1024]{1,0:T(8,128)(2,1)S(1)}, bf16[192,1024]{1,0:T(8,128)(2,1)S(1)}) custom-call(bf16[3,1024,80]{2,1,0:T(8,128)(2,1)S(1)} %copy-done.79, bf16[3,1024,80]{2,1,0:T(8,128)(2,1)S(1)} %delta.1.dox_ref, bf16[192,1024]{1,0:T(8,128)(2,1)S(1)} %bitcast.252, ...), custom_call_target="tpu_custom_call" | custom-call | flops 3221225472 | bytes 1048576 | tf_op jit(solution)/shard_map/attend_back/pallas_call | solution.py:286
  406.5 7.6 %attend_back.10 = (f32[192,1024]{1,0:T(8,128)S(1)}, bf16[192,1024]{1,0:T(8,128)(2,1)S(1)}, bf16[192,1024]{1,0:T(8,128)(2,1)S(1)}) custom-call(bf16[3,1024,80]{2,1,0:T(8,128)(2,1)S(1)} %copy-done.79, bf16[3,1024,80]{2,1,0:T(8,128)(2,1)S(1)} %delta.1.dox_ref, bf16[192,1024]{1,0:T(8,128)(2,1)S(1)} %bitcast.253, ...), custom_call_target="tpu_custom_call" | custom-call | flops 3221225472 | bytes 1048576 | tf_op jit(solution)/shard_map/attend_back/pallas_call | solution.py:286
  415.7 7.2 %attend_back.11 = (f32[192,1024]{1,0:T(8,128)S(1)}, bf16[192,1024]{1,0:T(8,128)(2,1)S(1)}, bf16[192,1024]{1,0:T(8,128)(2,1)S(1)}) custom-call(bf16[3,1024,80]{2,1,0:T(8,128)(2,1)S(1)} %copy-done.79, bf16[3,1024,80]{2,1,0:T(8,128)(2,1)S(1)} %delta.1.dox_ref, bf16[192,1024]{1,0:T(8,128)(2,1)S(1)} %bitcast.254, ...), custom_call_target="tpu_custom_call" | custom-call | flops 3221225472 | bytes 1048576 | tf_op jit(solution)/shard_map/attend_back/pallas_call | solution.py:286
  424.5 7.4 %attend_back.12 = (f32[192,1024]{1,0:T(8,128)S(1)}, bf16[192,1024]{1,0:T(8,128)(2,1)S(1)}, bf16[192,1024]{1,0:T(8,128)(2,1)S(1)}) custom-call(bf16[3,1024,80]{2,1,0:T(8,128)(2,1)S(1)} %copy-done.79, bf16[3,1024,80]{2,1,0:T(8,128)(2,1)S(1)} %delta.1.dox_ref, bf16[192,1024]{1,0:T(8,128)(2,1)S(1)} %bitcast.255, ...), custom_call_target="tpu_custom_call" | custom-call | flops 3221225472 | bytes 1048576 | tf_op jit(solution)/shard_map/attend_back/pallas_call | solution.py:286
  436.8 3.7 add_convert_fusion
  440.5 3.2 add_convert_fusion.1
  443.7 3.1 add_convert_fusion.2
  447.5 7.3 %concatenate.94 = bf16[8,96,2560]{2,1,0:T(8,128)(2,1)} concatenate(bf16[8,96,768]{2,1,0:T(8,128)(2,1)} %bitcast.293, bf16[8,96,768]{2,1,0:T(8,128)(2,1)} %bitcast.292, bf16[8,96,768]{2,1,0:T(8,128)(2,1)} %bitcast.291, bf16[8,96,192]{2,1,0:T(8,128)(2,1)S(1)} %bitcast.283, bf16[8,96,1]{2,1,0:T(8,128)(2,1)} %stack.232, bf16[8,96,1]{2,1,0:T(8,128)(2,1)} %stack.233, ...), dimensions={2} | concatenate | bytes 7864320 | tf_op jit(solution)/shard_map/concatenate | solution.py:591
  460.9 7.2 %attend_back.13 = (f32[192,1024]{1,0:T(8,128)S(1)}, bf16[192,1024]{1,0:T(8,128)(2,1)S(1)}, bf16[192,1024]{1,0:T(8,128)(2,1)S(1)}) custom-call(bf16[3,1024,80]{2,1,0:T(8,128)(2,1)S(1)} %copy-done.80, bf16[3,1024,80]{2,1,0:T(8,128)(2,1)S(1)} %copy-done.32, bf16[192,1024]{1,0:T(8,128)(2,1)S(1)} %bitcast.256, bf16[192,1024]{1,0:T(8,128)(2,1)S(1)} %pad_maximum_fusion.12.dot_ref, ...), custom_call_target="tpu_custom_call" | custom-call | flops 3221225472 | bytes 1048576 | tf_op jit(solution)/shard_map/attend_back/pallas_call | solution.py:286
  470.3 7.2 %attend_back.14 = (f32[192,1024]{1,0:T(8,128)S(1)}, bf16[192,1024]{1,0:T(8,128)(2,1)S(1)}, bf16[192,1024]{1,0:T(8,128)(2,1)S(1)}) custom-call(bf16[3,1024,80]{2,1,0:T(8,128)(2,1)S(1)} %copy-done.80, bf16[3,1024,80]{2,1,0:T(8,128)(2,1)S(1)} %copy-done.32, bf16[192,1024]{1,0:T(8,128)(2,1)S(1)} %bitcast.257, bf16[192,1024]{1,0:T(8,128)(2,1)S(1)} %pad_maximum_fusion.12.dot_ref, ...), custom_call_target="tpu_custom_call" | custom-call | flops 3221225472 | bytes 1048576 | tf_op jit(solution)/shard_map/attend_back/pallas_call | solution.py:286
  485.0 7.2 %attend_back.15 = (f32[192,1024]{1,0:T(8,128)S(1)}, bf16[192,1024]{1,0:T(8,128)(2,1)S(1)}, bf16[192,1024]{1,0:T(8,128)(2,1)S(1)}) custom-call(bf16[3,1024,80]{2,1,0:T(8,128)(2,1)S(1)} %copy-done.81, bf16[3,1024,80]{2,1,0:T(8,128)(2,1)S(1)} %copy-done.32, bf16[192,1024]{1,0:T(8,128)(2,1)S(1)} %bitcast.258, bf16[192,1024]{1,0:T(8,128)(2,1)S(1)} %pad_maximum_fusion.12.dot_ref, ...), custom_call_target="tpu_custom_call" | custom-call | flops 3221225472 | bytes 1048576 | tf_op jit(solution)/shard_map/attend_back/pallas_call | solution.py:286
  494.9 6.9 %collective-permute-done.66 = bf16[96,2560]{1,0:T(8,128)(2,1)S(1)} collective-permute-done((bf16[96,2560]{1,0:T(8,128)(2,1)}, bf16[96,2560]{1,0:T(8,128)(2,1)S(1)}, u32[]{:S(2)}, u32[]{:S(2)}) %collective-permute-start.66) | collective-permute-done | bytes 491552 | tf_op jit(solution)/shard_map/ppermute | solution.py:53
  503.6 12.5 %collective-permute-done.38 = bf16[384,1024]{1,0:T(8,128)(2,1)S(1)} collective-permute-done((bf16[384,1024]{1,0:T(8,128)(2,1)S(1)}, bf16[384,1024]{1,0:T(8,128)(2,1)S(1)}, u32[]{:S(2)}, u32[]{:S(2)}) %collective-permute-start.38) | collective-permute-done | bytes 786464 | tf_op jit(solution)/shard_map/ppermute | solution.py:53
  521.0 8.1 %collective-permute-done.67 = bf16[96,2560]{1,0:T(8,128)(2,1)S(1)} collective-permute-done((bf16[96,2560]{1,0:T(8,128)(2,1)S(1)}, bf16[96,2560]{1,0:T(8,128)(2,1)S(1)}, u32[]{:S(2)}, u32[]{:S(2)}) %collective-permute-start.67) | collective-permute-done | bytes 491552 | tf_op jit(solution)/shard_map/ppermute | solution.py:53
  529.8 7.2 %collective-permute-done.39 = bf16[384,1024]{1,0:T(8,128)(2,1)S(1)} collective-permute-done((bf16[384,1024]{1,0:T(8,128)(2,1)S(1)}, bf16[384,1024]{1,0:T(8,128)(2,1)S(1)}, u32[]{:S(2)}, u32[]{:S(2)}) %collective-permute-start.39) | collective-permute-done | bytes 786464 | tf_op jit(solution)/shard_map/ppermute | solution.py:53
  538.9 7.1 %collective-permute-done.43 = bf16[384,1024]{1,0:T(8,128)(2,1)S(1)} collective-permute-done((bf16[384,1024]{1,0:T(8,128)(2,1)S(1)}, bf16[384,1024]{1,0:T(8,128)(2,1)S(1)}, u32[]{:S(2)}, u32[]{:S(2)}) %collective-permute-start.43) | collective-permute-done | bytes 786464 | tf_op jit(solution)/shard_map/ppermute | solution.py:53
  547.5 9.1 %collective-permute-done.68 = bf16[96,2560]{1,0:T(8,128)(2,1)S(1)} collective-permute-done((bf16[96,2560]{1,0:T(8,128)(2,1)S(1)}, bf16[96,2560]{1,0:T(8,128)(2,1)S(1)}, u32[]{:S(2)}, u32[]{:S(2)}) %collective-permute-start.68) | collective-permute-done | bytes 491552 | tf_op jit(solution)/shard_map/ppermute | solution.py:53
  558.3 3.3 collective-permute-done.40
  561.6 8.7 %collective-permute-done.44 = bf16[384,1024]{1,0:T(8,128)(2,1)S(1)} collective-permute-done((bf16[384,1024]{1,0:T(8,128)(2,1)S(1)}, bf16[384,1024]{1,0:T(8,128)(2,1)S(1)}, u32[]{:S(2)}, u32[]{:S(2)}) %collective-permute-start.44) | collective-permute-done | bytes 786464 | tf_op jit(solution)/shard_map/ppermute | solution.py:53
  579.8 4.1 dot_general.99
  587.0 3.9 collective-permute-done.48
  603.4 3.4 collective-permute-done.54
  608.4 3.4 collective-permute-done.55.refs_1_
  (622 shorter events, 232.2 us)
Async XLA Ops:
  2.0 19.9 %collective-permute-start.4 = (bf16[96,576]{1,0:T(8,128)(2,1)S(1)}, bf16[96,576]{1,0:T(8,128)(2,1)S(1)}, u32[]{:S(2)}, u32[]{:S(2)}) collective-permute-start(bf16[96,576]{1,0:T(8,128)(2,1)S(1)} %pad_maximum_fusion.16.refs_0_), channel_id=1, source_target_pairs={{0,4},{8,0},{16,8},{24,16},{28,24},{20,28},{12,20},{4,12},{1,5},{9... | collective-permute-start | bytes 331784 | tf_op jit(solution)/shard_map/ppermute | solution.py:53
  5.0 18.6 %collective-permute-start.3 = (bf16[96,576]{1,0:T(8,128)(2,1)S(1)}, bf16[96,576]{1,0:T(8,128)(2,1)S(1)}, u32[]{:S(2)}, u32[]{:S(2)}) collective-permute-start(bf16[96,576]{1,0:T(8,128)(2,1)S(1)} %pad_maximum_fusion.16.refs_0_), channel_id=1, source_target_pairs={{0,8},{8,16},{16,24},{24,28},{28,20},{20,12},{12,4},{4,0},{1,9},{9... | collective-permute-start | bytes 331784 | tf_op jit(solution)/shard_map/ppermute | solution.py:53
  16.3 39.2 %collective-permute-start.21 = (bf16[96,3200]{1,0:T(8,128)(2,1)S(1)}, bf16[96,3200]{1,0:T(8,128)(2,1)}, u32[]{:S(2)}, u32[]{:S(2)}) collective-permute-start(bf16[96,3200]{1,0:T(8,128)(2,1)S(1)} %concatenate.81.refs_0_), channel_id=1, source_target_pairs={{0,8},{8,16},{16,24},{24,28},{28,20},{20,12},{12,4},{4,0},{1,9},{9... | collective-permute-start | bytes 1843208 | tf_op jit(solution)/shard_map/ppermute | solution.py:53
  18.3 38.8 %collective-permute-start.22 = (bf16[96,3200]{1,0:T(8,128)(2,1)S(1)}, bf16[96,3200]{1,0:T(8,128)(2,1)}, u32[]{:S(2)}, u32[]{:S(2)}) collective-permute-start(bf16[96,3200]{1,0:T(8,128)(2,1)S(1)} %concatenate.81.refs_0_), channel_id=1, source_target_pairs={{0,4},{8,0},{16,8},{24,16},{28,24},{20,28},{12,20},{4,12},{1,5},{9... | collective-permute-start | bytes 1843208 | tf_op jit(solution)/shard_map/ppermute | solution.py:53
  18.4 23.8 %collective-permute-start = (bf16[256,768]{1,0:T(8,128)(2,1)S(1)}, bf16[256,768]{1,0:T(8,128)(2,1)S(1)}, u32[]{:S(2)}, u32[]{:S(2)}) collective-permute-start(bf16[256,768]{1,0:T(8,128)(2,1)S(1)} %copy-done.57), channel_id=1, source_target_pairs={{0,2},{1,3},{2,0},{3,1},{4,6},{5,7},{6,4},{7,5},{8,10},{9,11},{10,... | collective-permute-start | bytes 1179656 | tf_op jit(solution)/shard_map/ppermute | solution.py:57
  21.9 13.8 %collective-permute-start.6 = (bf16[96,576]{1,0:T(8,128)(2,1)S(1)}, bf16[96,576]{1,0:T(8,128)(2,1)S(1)}, u32[]{:S(2)}, u32[]{:S(2)}) collective-permute-start(bf16[96,576]{1,0:T(8,128)(2,1)S(1)} %collective-permute-done.4.refs_2_), channel_id=1, source_target_pairs={{0,4},{8,0},{16,8},{24,16},{28,24},{20,28},{12,20},{4,12},{1,5},{9... | collective-permute-start | bytes 331784 | tf_op jit(solution)/shard_map/ppermute | solution.py:53
  36.7 21.0 %collective-permute-start.1 = (bf16[256,768]{1,0:T(8,128)(2,1)S(1)}, bf16[256,768]{1,0:T(8,128)(2,1)S(1)}, u32[]{:S(2)}, u32[]{:S(2)}) collective-permute-start(bf16[256,768]{1,0:T(8,128)(2,1)S(1)} %copy-done.57), channel_id=1, source_target_pairs={{0,1},{1,0},{2,3},{3,2},{4,5},{5,4},{6,7},{7,6},{8,9},{9,8},{10,11... | collective-permute-start | bytes 1179656 | tf_op jit(solution)/shard_map/ppermute | solution.py:57
  42.2 15.4 %collective-permute-start.2 = (bf16[256,768]{1,0:T(8,128)(2,1)S(1)}, bf16[256,768]{1,0:T(8,128)(2,1)S(1)}, u32[]{:S(2)}, u32[]{:S(2)}) collective-permute-start(bf16[256,768]{1,0:T(8,128)(2,1)S(1)} %collective-permute-done.refs_1_), channel_id=1, source_target_pairs={{0,1},{1,0},{2,3},{3,2},{4,5},{5,4},{6,7},{7,6},{8,9},{9,8},{10,11... | collective-permute-start | bytes 1179656 | tf_op jit(solution)/shard_map/ppermute | solution.py:57
  55.5 17.1 %collective-permute-start.23 = (bf16[96,3200]{1,0:T(8,128)(2,1)}, bf16[96,3200]{1,0:T(8,128)(2,1)S(1)}, u32[]{:S(2)}, u32[]{:S(2)}) collective-permute-start(bf16[96,3200]{1,0:T(8,128)(2,1)} %collective-permute-done.21.refs_1_), channel_id=1, source_target_pairs={{0,8},{8,16},{16,24},{24,28},{28,20},{20,12},{12,4},{4,0},{1,9},{9... | collective-permute-start | bytes 1843208 | tf_op jit(solution)/shard_map/ppermute | solution.py:53
  57.2 17.0 %collective-permute-start.24 = (bf16[96,3200]{1,0:T(8,128)(2,1)}, bf16[96,3200]{1,0:T(8,128)(2,1)S(1)}, u32[]{:S(2)}, u32[]{:S(2)}) collective-permute-start(bf16[96,3200]{1,0:T(8,128)(2,1)} %collective-permute-done.22.refs_2_), channel_id=1, source_target_pairs={{0,4},{8,0},{16,8},{24,16},{28,24},{20,28},{12,20},{4,12},{1,5},{9... | collective-permute-start | bytes 1843208 | tf_op jit(solution)/shard_map/ppermute | solution.py:53
  62.8 28.2 %collective-permute-start.12 = (bf16[384,1024]{1,0:T(8,128)(2,1)S(1)}, bf16[384,1024]{1,0:T(8,128)(2,1)S(1)}, u32[]{:S(2)}, u32[]{:S(2)}) collective-permute-start(bf16[384,1024]{1,0:T(8,128)(2,1)S(1)} %pad_maximum_fusion.2), channel_id=1, source_target_pairs={{0,4},{8,0},{16,8},{24,16},{28,24},{20,28},{12,20},{4,12},{1,5},{9... | collective-permute-start | bytes 2359304 | tf_op jit(solution)/shard_map/ppermute | solution.py:53
  63.2 28.3 %collective-permute-start.11 = (bf16[384,1024]{1,0:T(8,128)(2,1)S(1)}, bf16[384,1024]{1,0:T(8,128)(2,1)S(1)}, u32[]{:S(2)}, u32[]{:S(2)}) collective-permute-start(bf16[384,1024]{1,0:T(8,128)(2,1)S(1)} %pad_maximum_fusion.2), channel_id=1, source_target_pairs={{0,8},{8,16},{16,24},{24,28},{28,20},{20,12},{12,4},{4,0},{1,9},{9... | collective-permute-start | bytes 2359304 | tf_op jit(solution)/shard_map/ppermute | solution.py:53
  72.6 30.0 %collective-permute-start.25 = (bf16[96,3200]{1,0:T(8,128)(2,1)S(1)}, bf16[96,3200]{1,0:T(8,128)(2,1)S(1)}, u32[]{:S(2)}, u32[]{:S(2)}) collective-permute-start(bf16[96,3200]{1,0:T(8,128)(2,1)S(1)} %collective-permute-done.23.refs_3_), channel_id=1, source_target_pairs={{0,8},{8,16},{16,24},{24,28},{28,20},{20,12},{12,4},{4,0},{1,9},{9... | collective-permute-start | bytes 1843208 | tf_op jit(solution)/shard_map/ppermute | solution.py:53
  74.2 30.1 %collective-permute-start.26 = (bf16[96,3200]{1,0:T(8,128)(2,1)S(1)}, bf16[96,3200]{1,0:T(8,128)(2,1)S(1)}, u32[]{:S(2)}, u32[]{:S(2)}) collective-permute-start(bf16[96,3200]{1,0:T(8,128)(2,1)S(1)} %collective-permute-done.24.refs_4_), channel_id=1, source_target_pairs={{0,4},{8,0},{16,8},{24,16},{28,24},{20,28},{12,20},{4,12},{1,5},{9... | collective-permute-start | bytes 1843208 | tf_op jit(solution)/shard_map/ppermute | solution.py:53
  91.0 30.1 %collective-permute-start.14 = (bf16[384,1024]{1,0:T(8,128)(2,1)S(1)}, bf16[384,1024]{1,0:T(8,128)(2,1)}, u32[]{:S(2)}, u32[]{:S(2)}) collective-permute-start(bf16[384,1024]{1,0:T(8,128)(2,1)S(1)} %collective-permute-done.12), channel_id=1, source_target_pairs={{0,4},{8,0},{16,8},{24,16},{28,24},{20,28},{12,20},{4,12},{1,5},{9... | collective-permute-start | bytes 2359304 | tf_op jit(solution)/shard_map/ppermute | solution.py:53
  91.5 30.1 %collective-permute-start.13 = (bf16[384,1024]{1,0:T(8,128)(2,1)S(1)}, bf16[384,1024]{1,0:T(8,128)(2,1)S(1)}, u32[]{:S(2)}, u32[]{:S(2)}) collective-permute-start(bf16[384,1024]{1,0:T(8,128)(2,1)S(1)} %collective-permute-done.11), channel_id=1, source_target_pairs={{0,8},{8,16},{16,24},{24,28},{28,20},{20,12},{12,4},{4,0},{1,9},{9... | collective-permute-start | bytes 2359304 | tf_op jit(solution)/shard_map/ppermute | solution.py:53
  102.6 23.4 %collective-permute-start.27 = (bf16[48,3200]{1,0:T(8,128)(2,1)S(1)}, bf16[48,3200]{1,0:T(8,128)(2,1)S(1)}, u32[]{:S(2)}, u32[]{:S(2)}) collective-permute-start(bf16[48,3200]{1,0:T(8,128)(2,1)S(1)} %slice.363), channel_id=1, source_target_pairs={{0,8},{8,16},{16,24},{24,28},{28,20},{20,12},{12,4},{4,0},{1,9},{9... | collective-permute-start | bytes 921608 | tf_op jit(solution)/shard_map/ppermute | solution.py:53
  104.3 23.3 %collective-permute-start.28 = (bf16[48,3200]{1,0:T(8,128)(2,1)S(1)}, bf16[48,3200]{1,0:T(8,128)(2,1)S(1)}, u32[]{:S(2)}, u32[]{:S(2)}) collective-permute-start(bf16[48,3200]{1,0:T(8,128)(2,1)S(1)} %slice.364), channel_id=1, source_target_pairs={{0,4},{8,0},{16,8},{24,16},{28,24},{20,28},{12,20},{4,12},{1,5},{9... | collective-permute-start | bytes 921608 | tf_op jit(solution)/shard_map/ppermute | solution.py:53
  121.1 20.6 %collective-permute-start.16 = (bf16[384,1024]{1,0:T(8,128)(2,1)}, bf16[384,1024]{1,0:T(8,128)(2,1)}, u32[]{:S(2)}, u32[]{:S(2)}) collective-permute-start(bf16[384,1024]{1,0:T(8,128)(2,1)} %collective-permute-done.14), channel_id=1, source_target_pairs={{0,4},{8,0},{16,8},{24,16},{28,24},{20,28},{12,20},{4,12},{1,5},{9... | collective-permute-start | bytes 2359304 | tf_op jit(solution)/shard_map/ppermute | solution.py:53
  121.6 17.3 %collective-permute-start.15 = (bf16[384,1024]{1,0:T(8,128)(2,1)S(1)}, bf16[384,1024]{1,0:T(8,128)(2,1)}, u32[]{:S(2)}, u32[]{:S(2)}) collective-permute-start(bf16[384,1024]{1,0:T(8,128)(2,1)S(1)} %collective-permute-done.13), channel_id=1, source_target_pairs={{0,8},{8,16},{16,24},{24,28},{28,20},{20,12},{12,4},{4,0},{1,9},{9... | collective-permute-start | bytes 2359304 | tf_op jit(solution)/shard_map/ppermute | solution.py:53
  140.1 16.6 %collective-permute-start.17 = (bf16[192,1024]{1,0:T(8,128)(2,1)S(1)}, bf16[192,1024]{1,0:T(8,128)(2,1)S(1)}, u32[]{:S(2)}, u32[]{:S(2)}) collective-permute-start(bf16[192,1024]{1,0:T(8,128)(2,1)S(1)} %get-tuple-element.152.refs_2_.refs_3_.k_ref), channel_id=1, source_target_pairs={{0,8},{8,16},{16,24},{24,28},{28,20},{20,12},{12,4},{4,0},{1,9},{9... | collective-permute-start | bytes 1179656 | tf_op jit(solution)/shard_map/ppermute | solution.py:53
  142.9 13.8 %collective-permute-start.18 = (bf16[192,1024]{1,0:T(8,128)(2,1)S(1)}, bf16[192,1024]{1,0:T(8,128)(2,1)S(1)}, u32[]{:S(2)}, u32[]{:S(2)}) collective-permute-start(bf16[192,1024]{1,0:T(8,128)(2,1)S(1)} %get-tuple-element.149.refs_6_.refs_16_.v_ref), channel_id=1, source_target_pairs={{0,4},{8,0},{16,8},{24,16},{28,24},{20,28},{12,20},{4,12},{1,5},{9... | collective-permute-start | bytes 1179656 | tf_op jit(solution)/shard_map/ppermute | solution.py:53
  180.8 28.8 %collective-permute-start.29 = (bf16[768,768]{1,0:T(8,128)(2,1)S(1)}, bf16[768,768]{1,0:T(8,128)(2,1)S(1)}, u32[]{:S(2)}, u32[]{:S(2)}) collective-permute-start(bf16[768,768]{1,0:T(8,128)(2,1)S(1)} %get-tuple-element.109), channel_id=1, source_target_pairs={{0,2},{1,3},{2,0},{3,1},{4,6},{5,7},{6,4},{7,5},{8,10},{9,11},{10,... | collective-permute-start | bytes 3538952 | tf_op jit(solution)/shard_map/ppermute | solution.py:57
  182.3 52.7 %collective-permute-start.30 = (bf16[768,768]{1,0:T(8,128)(2,1)S(1)}, bf16[768,768]{1,0:T(8,128)(2,1)}, u32[]{:S(2)}, u32[]{:S(2)}) collective-permute-start(bf16[768,768]{1,0:T(8,128)(2,1)S(1)} %get-tuple-element.108), channel_id=1, source_target_pairs={{0,2},{1,3},{2,0},{3,1},{4,6},{5,7},{6,4},{7,5},{8,10},{9,11},{10,... | collective-permute-start | bytes 3538952 | tf_op jit(solution)/shard_map/ppermute | solution.py:57
  182.8 76.9 %collective-permute-start.31 = (bf16[768,768]{1,0:T(8,128)(2,1)S(1)}, bf16[768,768]{1,0:T(8,128)(2,1)}, u32[]{:S(2)}, u32[]{:S(2)}) collective-permute-start(bf16[768,768]{1,0:T(8,128)(2,1)S(1)} %get-tuple-element.107), channel_id=1, source_target_pairs={{0,2},{1,3},{2,0},{3,1},{4,6},{5,7},{6,4},{7,5},{8,10},{9,11},{10,... | collective-permute-start | bytes 3538952 | tf_op jit(solution)/shard_map/ppermute | solution.py:57
  303.0 133.8 %collective-permute-start.59 = (bf16[768,768]{1,0:T(8,128)(2,1)}, bf16[768,768]{1,0:T(8,128)(2,1)}, u32[]{:S(2)}, u32[]{:S(2)}) collective-permute-start(bf16[768,768]{1,0:T(8,128)(2,1)} %convolution_convert_fusion), channel_id=1, source_target_pairs={{0,2},{1,3},{2,0},{3,1},{4,6},{5,7},{6,4},{7,5},{8,10},{9,11},{10,... | collective-permute-start | bytes 3538952 | tf_op jit(solution)/shard_map/ppermute | solution.py:57
  304.5 135.9 %collective-permute-start.58 = (bf16[768,768]{1,0:T(8,128)(2,1)}, bf16[768,768]{1,0:T(8,128)(2,1)}, u32[]{:S(2)}, u32[]{:S(2)}) collective-permute-start(bf16[768,768]{1,0:T(8,128)(2,1)} %convolution_convert_fusion.1), channel_id=1, source_target_pairs={{0,2},{1,3},{2,0},{3,1},{4,6},{5,7},{6,4},{7,5},{8,10},{9,11},{10,... | collective-permute-start | bytes 3538952 | tf_op jit(solution)/shard_map/ppermute | solution.py:57
  306.9 136.8 %collective-permute-start.57 = (bf16[768,768]{1,0:T(8,128)(2,1)}, bf16[768,768]{1,0:T(8,128)(2,1)}, u32[]{:S(2)}, u32[]{:S(2)}) collective-permute-start(bf16[768,768]{1,0:T(8,128)(2,1)} %convolution_convert_fusion.2), channel_id=1, source_target_pairs={{0,2},{1,3},{2,0},{3,1},{4,6},{5,7},{6,4},{7,5},{8,10},{9,11},{10,... | collective-permute-start | bytes 3538952 | tf_op jit(solution)/shard_map/ppermute | solution.py:57
  313.6 73.2 %collective-permute-start.36 = (bf16[192,512]{1,0:T(8,128)(2,1)S(1)}, bf16[192,512]{1,0:T(8,128)(2,1)S(1)}, u32[]{:S(2)}, u32[]{:S(2)}) collective-permute-start(bf16[192,512]{1,0:T(8,128)(2,1)S(1)} %convolution_convert_fusion.5), channel_id=1, source_target_pairs={{0,2},{1,3},{2,0},{3,1},{4,6},{5,7},{6,4},{7,5},{8,10},{9,11},{10,... | collective-permute-start | bytes 589832 | tf_op jit(solution)/shard_map/ppermute | solution.py:57
  314.8 119.5 %collective-permute-start.60 = (bf16[768,192]{0,1:T(8,128)(2,1)S(1)}, bf16[768,192]{0,1:T(8,128)(2,1)S(1)}, u32[]{:S(2)}, u32[]{:S(2)}) collective-permute-start(bf16[768,192]{0,1:T(8,128)(2,1)S(1)} %convolution_convert_fusion.4), channel_id=1, source_target_pairs={{0,2},{1,3},{2,0},{3,1},{4,6},{5,7},{6,4},{7,5},{8,10},{9,11},{10,... | collective-permute-start | bytes 884744 | tf_op jit(solution)/shard_map/ppermute | solution.py:57
  468.4 13.7 %collective-permute-start.62 = (bf16[96,2560]{1,0:T(8,128)(2,1)S(1)}, bf16[96,2560]{1,0:T(8,128)(2,1)S(1)}, u32[]{:S(2)}, u32[]{:S(2)}) collective-permute-start(bf16[96,2560]{1,0:T(8,128)(2,1)S(1)} %pad_maximum_fusion.6), channel_id=1, source_target_pairs={{0,8},{8,16},{16,24},{24,28},{28,20},{20,12},{12,4},{4,0},{1,9},{9... | collective-permute-start | bytes 1474568 | tf_op jit(solution)/shard_map/ppermute | solution.py:53
  477.6 14.7 %collective-permute-start.37 = (bf16[192,1024]{1,0:T(8,128)(2,1)S(1)}, bf16[192,1024]{1,0:T(8,128)(2,1)S(1)}, u32[]{:S(2)}, u32[]{:S(2)}) collective-permute-start(bf16[192,1024]{1,0:T(8,128)(2,1)S(1)} %copy-done.85), channel_id=1, source_target_pairs={{0,8},{8,16},{16,24},{24,28},{28,20},{20,12},{12,4},{4,0},{1,9},{9... | collective-permute-start | bytes 1179656 | tf_op jit(solution)/shard_map/ppermute | solution.py:53
  479.2 15.1 %collective-permute-start.41 = (bf16[192,1024]{1,0:T(8,128)(2,1)S(1)}, bf16[192,1024]{1,0:T(8,128)(2,1)S(1)}, u32[]{:S(2)}, u32[]{:S(2)}) collective-permute-start(bf16[192,1024]{1,0:T(8,128)(2,1)S(1)} %copy-done.83), channel_id=1, source_target_pairs={{0,4},{8,0},{16,8},{24,16},{28,24},{20,28},{12,20},{4,12},{1,5},{9... | collective-permute-start | bytes 1179656 | tf_op jit(solution)/shard_map/ppermute | solution.py:53
  480.5 21.3 %collective-permute-start.66 = (bf16[96,2560]{1,0:T(8,128)(2,1)}, bf16[96,2560]{1,0:T(8,128)(2,1)S(1)}, u32[]{:S(2)}, u32[]{:S(2)}) collective-permute-start(bf16[96,2560]{1,0:T(8,128)(2,1)} %pad_maximum_fusion.7), channel_id=1, source_target_pairs={{0,4},{8,0},{16,8},{24,16},{28,24},{20,28},{12,20},{4,12},{1,5},{9... | collective-permute-start | bytes 1474568 | tf_op jit(solution)/shard_map/ppermute | solution.py:53
  483.0 18.8 %collective-permute-start.63 = (bf16[96,2560]{1,0:T(8,128)(2,1)}, bf16[96,2560]{1,0:T(8,128)(2,1)}, u32[]{:S(2)}, u32[]{:S(2)}) collective-permute-start(bf16[96,2560]{1,0:T(8,128)(2,1)} %fusion.5), channel_id=1, source_target_pairs={{0,8},{8,16},{16,24},{24,28},{28,20},{20,12},{12,4},{4,0},{1,9},{9... | collective-permute-start | bytes 1474568 | tf_op jit(solution)/shard_map/ppermute | solution.py:53
  492.5 23.6 %collective-permute-start.38 = (bf16[384,1024]{1,0:T(8,128)(2,1)S(1)}, bf16[384,1024]{1,0:T(8,128)(2,1)S(1)}, u32[]{:S(2)}, u32[]{:S(2)}) collective-permute-start(bf16[384,1024]{1,0:T(8,128)(2,1)S(1)} %pad_maximum_fusion.3), channel_id=1, source_target_pairs={{0,8},{8,16},{16,24},{24,28},{28,20},{20,12},{12,4},{4,0},{1,9},{9... | collective-permute-start | bytes 2359304 | tf_op jit(solution)/shard_map/ppermute | solution.py:53
  494.5 24.1 %collective-permute-start.42 = (bf16[384,1024]{1,0:T(8,128)(2,1)S(1)}, bf16[384,1024]{1,0:T(8,128)(2,1)S(1)}, u32[]{:S(2)}, u32[]{:S(2)}) collective-permute-start(bf16[384,1024]{1,0:T(8,128)(2,1)S(1)} %pad_maximum_fusion.4), channel_id=1, source_target_pairs={{0,4},{8,0},{16,8},{24,16},{28,24},{20,28},{12,20},{4,12},{1,5},{9... | collective-permute-start | bytes 2359304 | tf_op jit(solution)/shard_map/ppermute | solution.py:53
  503.1 26.1 %collective-permute-start.67 = (bf16[96,2560]{1,0:T(8,128)(2,1)S(1)}, bf16[96,2560]{1,0:T(8,128)(2,1)S(1)}, u32[]{:S(2)}, u32[]{:S(2)}) collective-permute-start(bf16[96,2560]{1,0:T(8,128)(2,1)S(1)} %get-tuple-element.111), channel_id=1, source_target_pairs={{0,4},{8,0},{16,8},{24,16},{28,24},{20,28},{12,20},{4,12},{1,5},{9... | collective-permute-start | bytes 1474568 | tf_op jit(solution)/shard_map/ppermute | solution.py:53
  516.4 20.5 %collective-permute-start.39 = (bf16[384,1024]{1,0:T(8,128)(2,1)S(1)}, bf16[384,1024]{1,0:T(8,128)(2,1)S(1)}, u32[]{:S(2)}, u32[]{:S(2)}) collective-permute-start(bf16[384,1024]{1,0:T(8,128)(2,1)S(1)} %maximum_add_fusion.1), channel_id=1, source_target_pairs={{0,8},{8,16},{16,24},{24,28},{28,20},{20,12},{12,4},{4,0},{1,9},{9... | collective-permute-start | bytes 2359304 | tf_op jit(solution)/shard_map/ppermute | solution.py:53
  518.9 27.1 %collective-permute-start.43 = (bf16[384,1024]{1,0:T(8,128)(2,1)S(1)}, bf16[384,1024]{1,0:T(8,128)(2,1)S(1)}, u32[]{:S(2)}, u32[]{:S(2)}) collective-permute-start(bf16[384,1024]{1,0:T(8,128)(2,1)S(1)} %maximum_add_fusion.3), channel_id=1, source_target_pairs={{0,4},{8,0},{16,8},{24,16},{28,24},{20,28},{12,20},{4,12},{1,5},{9... | collective-permute-start | bytes 2359304 | tf_op jit(solution)/shard_map/ppermute | solution.py:53
  519.4 28.0 %collective-permute-start.64 = (bf16[96,2560]{1,0:T(8,128)(2,1)S(1)}, bf16[96,2560]{1,0:T(8,128)(2,1)S(1)}, u32[]{:S(2)}, u32[]{:S(2)}) collective-permute-start(bf16[96,2560]{1,0:T(8,128)(2,1)S(1)} %get-tuple-element.110), channel_id=1, source_target_pairs={{0,8},{8,16},{16,24},{24,28},{28,20},{20,12},{12,4},{4,0},{1,9},{9... | collective-permute-start | bytes 1474568 | tf_op jit(solution)/shard_map/ppermute | solution.py:53
  529.3 27.3 %collective-permute-start.68 = (bf16[96,2560]{1,0:T(8,128)(2,1)S(1)}, bf16[96,2560]{1,0:T(8,128)(2,1)S(1)}, u32[]{:S(2)}, u32[]{:S(2)}) collective-permute-start(bf16[96,2560]{1,0:T(8,128)(2,1)S(1)} %fusion.4), channel_id=1, source_target_pairs={{0,4},{8,0},{16,8},{24,16},{28,24},{20,28},{12,20},{4,12},{1,5},{9... | collective-permute-start | bytes 1474568 | tf_op jit(solution)/shard_map/ppermute | solution.py:53
  537.3 24.3 %collective-permute-start.40 = (bf16[384,1024]{1,0:T(8,128)(2,1)S(1)}, bf16[384,1024]{1,0:T(8,128)(2,1)S(1)}, u32[]{:S(2)}, u32[]{:S(2)}) collective-permute-start(bf16[384,1024]{1,0:T(8,128)(2,1)S(1)} %maximum_add_fusion), channel_id=1, source_target_pairs={{0,8},{8,16},{16,24},{24,28},{28,20},{20,12},{12,4},{4,0},{1,9},{9... | collective-permute-start | bytes 2359304 | tf_op jit(solution)/shard_map/ppermute | solution.py:53
  546.3 24.0 %collective-permute-start.44 = (bf16[384,1024]{1,0:T(8,128)(2,1)S(1)}, bf16[384,1024]{1,0:T(8,128)(2,1)S(1)}, u32[]{:S(2)}, u32[]{:S(2)}) collective-permute-start(bf16[384,1024]{1,0:T(8,128)(2,1)S(1)} %maximum_add_fusion.2), channel_id=1, source_target_pairs={{0,4},{8,0},{16,8},{24,16},{28,24},{20,28},{12,20},{4,12},{1,5},{9... | collective-permute-start | bytes 2359304 | tf_op jit(solution)/shard_map/ppermute | solution.py:53
  556.7 45.6 %collective-permute-start.69 = (bf16[96,2560]{1,0:T(8,128)(2,1)S(1)}, bf16[96,2560]{1,0:T(8,128)(2,1)S(1)}, u32[]{:S(2)}, u32[]{:S(2)}) collective-permute-start(bf16[96,2560]{1,0:T(8,128)(2,1)S(1)} %fusion.8.refs_0_), channel_id=1, source_target_pairs={{0,2},{1,3},{2,0},{3,1},{4,6},{5,7},{6,4},{7,5},{8,10},{9,11},{10,... | collective-permute-start | bytes 1474568 | tf_op jit(solution)/shard_map/ppermute | solution.py:57
  597.5 14.5 %collective-permute-start.45 = (bf16[2,256,768]{2,1,0:T(8,128)(2,1)S(1)}, bf16[2,256,768]{2,1,0:T(8,128)(2,1)}, u32[]{:S(2)}, u32[]{:S(2)}) collective-permute-start(bf16[2,256,768]{2,1,0:T(8,128)(2,1)S(1)} %fusion.16), channel_id=1, source_target_pairs={{0,1},{1,0},{2,3},{3,2},{4,5},{5,4},{6,7},{7,6},{8,9},{9,8},{10,11... | collective-permute-start | bytes 2359304 | tf_op jit(solution)/shard_map/ppermute | solution.py:57
  603.4 18.1 %collective-permute-start.70 = (bf16[2,96,2560]{2,1,0:T(8,128)(2,1)}, bf16[2,96,2560]{2,1,0:T(8,128)(2,1)}, u32[]{:S(2)}, u32[]{:S(2)}) collective-permute-start(bf16[2,96,2560]{2,1,0:T(8,128)(2,1)} %pad_maximum_fusion.1), channel_id=1, source_target_pairs={{0,1},{1,0},{2,3},{3,2},{4,5},{5,4},{6,7},{7,6},{8,9},{9,8},{10,11... | collective-permute-start | bytes 2949128 | tf_op jit(solution)/shard_map/ppermute | solution.py:57
  614.6 27.1 %collective-permute-start.46 = (bf16[256,768]{1,0:T(8,128)(2,1)}, bf16[256,768]{1,0:T(8,128)(2,1)}, u32[]{:S(2)}, u32[]{:S(2)}) collective-permute-start(bf16[256,768]{1,0:T(8,128)(2,1)} %fusion.23), channel_id=1, source_target_pairs={{0,2},{1,3},{2,0},{3,1},{4,6},{5,7},{6,4},{7,5},{8,10},{9,11},{10,... | collective-permute-start | bytes 1179656 | tf_op jit(solution)/shard_map/ppermute | solution.py:57
  (182 other events, 1896.0 us)
